TPU v7x, 32 devices: a whole 2x2x4 slice. The times are simulated.
32 devices in a mesh: groups: 2 (over y), leaf: 4 (over z), sub: 2 (over x), rep: 2 (over core).
Axes of the slice: x: 2, y: 2, z: 4, core: 2. Of those that a mesh axis runs over, the one named last changes fastest.
Arguments:
- coords: float32 [3, 32, 8, 256], P(None, ('groups', 'leaf'), 'sub'), parts along dimension 1, may hold values from 0 to 16, as said below
- vector: float32 [8, 32, 8, 256], P('rep', ('groups', 'leaf'), 'sub'), parts along dimension 1, may hold values from -6 to 6
Outputs:
- potential: float32 [8, 32, 8, 256], P('rep', ('groups', 'leaf'), 'sub'), parts along dimension 1
There are 2 independent parts, one for each index of `groups`. A program takes and returns all parts, laid end to end along the dimension named above; each array names one. Nothing has to cross between parts.
Inputs may be any that keep to these rules, and one draw needn't show every extreme that they name: `coords`: point a of leaf box (i, j) has its first coordinate in [i, i + 1), its second in [j, j + 1) and its third in [0, 1).
All inputs are finite; a program needn't handle non-finite values.
Results may differ from a plain program's by a relative error of at most 0.0003.
Values sent between devices are 32-bit elements; how exact they have to be, the bound alone decides.
A program may use at most 64 MiB of HBM per device.

v0:
```python
import jax
import jax.numpy as jnp
import numpy as np
from jax import lax
from jax.sharding import PartitionSpec as P

QUAD_WEIGHT = 1.0 / 64.0
SMOOTHING = 0.01
HIGHEST = lax.Precision.HIGHEST
CHEB_NODES = np.cos((2.0 * np.arange(4) + 1.0) * np.pi / 8.0)


def extended(x, sides, width):
    for axis, dim in sides:
        peers, length = (lax.axis_size(axis), x.shape[dim])
        up = [(i, (i + 1) % peers) for i in range(peers - 1)]
        down = [(j, i) for i, j in up]
        last = lax.slice_in_dim(x, length - width, length, axis=dim)
        leading = lax.slice_in_dim(x, 0, width, axis=dim)
        before = lax.ppermute(last, axis, up)
        after = lax.ppermute(leading, axis, down)
        x = jnp.concatenate([before, x, after], axis=dim)
    return x


def poly_values(points):
    second = 2.0 * points * points - 1.0
    third = 2.0 * points * second - points
    return (points, second, third)


def cheb_numpy(values):
    nodes_one, nodes_two, nodes_three = poly_values(CHEB_NODES)
    first, second, third = poly_values(values)
    return 0.25 + 0.5 * (
        first[..., None] * nodes_one
        + second[..., None] * nodes_two
        + third[..., None] * nodes_three
    )


def chebyshev(values):
    nodes_one, nodes_two, nodes_three = poly_values(CHEB_NODES)
    first, second, third = poly_values(values)
    return 0.25 + 0.5 * (
        first[..., None] * jnp.asarray(nodes_one, jnp.float32)
        + second[..., None] * jnp.asarray(nodes_two, jnp.float32)
        + third[..., None] * jnp.asarray(nodes_three, jnp.float32)
    )


def transfer_table():
    halves = [cheb_numpy((CHEB_NODES + 2.0 * side_bit - 1.0) / 2.0) for side_bit in range(2)]
    same_node = np.eye(4)
    blocks = [
        [
            (
                halves[row_bit][:, None, None, :, None, None]
                * halves[col_bit][None, :, None, None, :, None]
                * same_node[None, None, :, None, None, :]
            ).reshape(64, 64)
            for col_bit in range(2)
        ]
        for row_bit in range(2)
    ]
    return np.array(blocks)


def couple_table(tree_level):
    box_width = 2.0**tree_level
    across = 0.5 * box_width * CHEB_NODES
    height = 0.5 + 0.5 * CHEB_NODES
    target = np.stack(np.meshgrid(across, across, height, indexing="ij"), -1).reshape(64, 3)
    table_rows = []
    for row_shift in range(-3, 4):
        table_line = []
        for col_shift in range(-3, 4):
            source = target + np.array([row_shift * box_width, col_shift * box_width, 0.0])
            spacing = target[:, None, :] - source[None, :, :]
            values = QUAD_WEIGHT / np.sqrt(np.sum(spacing * spacing, -1) + SMOOTHING)
            far_flag = float(max(abs(row_shift), abs(col_shift)) >= 2)
            table_line.append(values * far_flag)
        table_rows.append(table_line)
    return np.array(table_rows)


def near_leaf(target, source):
    squares = jnp.zeros((source.shape[1], source.shape[2], target.shape[1]), jnp.float32)
    for axis_id in range(3):
        spacing = source[axis_id][:, :, None] - target[axis_id][None, None, :]
        squares = squares + spacing * spacing
    kernel = QUAD_WEIGHT * lax.rsqrt(squares + SMOOTHING)
    return jnp.einsum("cnb,nba->ca", source[3:], kernel, precision=HIGHEST)


def near_block(padded):
    stack_depth = padded.shape[0]
    rows_here = padded.shape[1] - 2
    cols_here = padded.shape[2] - 2
    point_count = padded.shape[3]
    pair_rows = cols_here // 2
    zero_index = jnp.zeros((), jnp.int32)

    def per_pair(pair_id):
        row_at = pair_id // pair_rows
        col_at = 2 * (pair_id % pair_rows)
        window = lax.dynamic_slice(
            padded, (zero_index, row_at, col_at, zero_index), (stack_depth, 3, 4, point_count)
        )
        targets = jnp.stack([window[:3, 1, 1], window[:3, 1, 2]])
        sources = jnp.stack(
            [
                jnp.stack(
                    [
                        window[:, row_shift, col_shift + offset]
                        for row_shift in range(3)
                        for col_shift in range(3)
                    ],
                    1,
                )
                for offset in range(2)
            ]
        )
        return jax.vmap(near_leaf)(targets, sources)

    result = lax.map(per_pair, jnp.arange(rows_here * pair_rows, dtype=jnp.int32))
    result = result.reshape(rows_here, cols_here, stack_depth - 3, point_count)
    return jnp.transpose(result, (2, 0, 1, 3))


def leaf_basis(coords, start_row, start_col):
    rows_here = coords.shape[1]
    cols_here = coords.shape[2]
    row_mid = (start_row + jnp.arange(rows_here, dtype=jnp.int32)).astype(jnp.float32)[
        :, None, None
    ] + 0.5
    col_mid = (start_col + jnp.arange(cols_here, dtype=jnp.int32)).astype(jnp.float32)[
        None, :, None
    ] + 0.5
    along_x = jnp.moveaxis(chebyshev(2.0 * (coords[0] - row_mid)), -1, 2)
    along_y = jnp.moveaxis(chebyshev(2.0 * (coords[1] - col_mid)), -1, 2)
    along_z = jnp.moveaxis(chebyshev(2.0 * coords[2] - 1.0), -1, 2)
    product = (
        along_x[:, :, :, None, None, :]
        * along_y[:, :, None, :, None, :]
        * along_z[:, :, None, None, :, :]
    )
    return product.reshape(rows_here, cols_here, 64, coords.shape[3])


def make_moments(basis_table, vector):
    return jnp.einsum("ijra,cija->ijcr", basis_table, vector, precision=HIGHEST)


def evaluate_far(basis_table, summed):
    return jnp.einsum("ijra,ijcr->cija", basis_table, summed, precision=HIGHEST)


def upward(moments):
    rows_here, cols_here, column_count = (moments.shape[0], moments.shape[1], moments.shape[2])
    blocks = moments.reshape(rows_here // 2, 2, cols_here // 2, 2, column_count, 64)
    table = jnp.asarray(transfer_table(), jnp.float32)
    return jnp.einsum("idjecs,desr->ijcr", blocks, table, precision=HIGHEST)


def downward(parent_local):
    rows_here, cols_here, column_count = (
        parent_local.shape[0],
        parent_local.shape[1],
        parent_local.shape[2],
    )
    table = jnp.asarray(transfer_table(), jnp.float32)
    children = jnp.einsum("ijcr,desr->idjecs", parent_local, table, precision=HIGHEST)
    return children.reshape(2 * rows_here, 2 * cols_here, column_count, 64)


def coupling_block(window, start_row, start_col, tree_level):
    rows_here = window.shape[0] - 6
    cols_here = window.shape[1] - 6
    offsets = jnp.arange(7, dtype=jnp.int32) - 3
    row_ids = start_row + jnp.arange(rows_here, dtype=jnp.int32)
    col_ids = start_col + jnp.arange(cols_here, dtype=jnp.int32)
    row_ok = (
        jnp.abs(
            jnp.floor_divide(row_ids[None, :] + offsets[:, None], 2)
            - jnp.floor_divide(row_ids, 2)[None, :]
        )
        <= 1
    )
    col_ok = (
        jnp.abs(
            jnp.floor_divide(col_ids[None, :] + offsets[:, None], 2)
            - jnp.floor_divide(col_ids, 2)[None, :]
        )
        <= 1
    )
    table = jnp.asarray(couple_table(tree_level), jnp.float32)
    total = jnp.zeros((rows_here, cols_here, window.shape[2], 64), jnp.float32)
    for row_shift in range(7):
        slab = jnp.stack(
            [
                window[row_shift : row_shift + rows_here, col_shift : col_shift + cols_here]
                for col_shift in range(7)
            ]
        )
        weight = (row_ok[row_shift][None, :, None] & col_ok[:, None, :]).astype(jnp.float32)
        total = total + jnp.einsum(
            "vxycs,vrs->xycr",
            slab * weight[:, :, :, None, None],
            table[row_shift],
            precision=HIGHEST,
        )
    return total


def local(coords, vector):
    leaf_side = coords.shape[1]
    column_count = vector.shape[0]
    sub_count = lax.axis_size("sub")
    leaf_total = lax.axis_size("leaf")
    leaf_at = lax.axis_index("leaf")
    sub_at = lax.axis_index("sub")
    top_level = (leaf_side * sub_count).bit_length() - 1
    base_level = leaf_side.bit_length() - 1
    zero_index = jnp.zeros((), jnp.int32)
    half_side = leaf_side // 2
    all_columns = lax.all_to_all(vector, "rep", split_axis=1, concat_axis=0, tiled=True)
    own_start = lax.axis_index("rep") * half_side
    own_coords = lax.dynamic_slice_in_dim(coords, own_start, half_side, 1)
    padded = extended(
        jnp.concatenate([own_coords, all_columns], 0), ((("leaf", "rep"), 1), ("sub", 2)), 1
    )
    near_part = lax.all_to_all(near_block(padded), "rep", split_axis=0, concat_axis=1, tiled=True)
    row_start = leaf_at * leaf_side
    col_start = sub_at * leaf_side
    basis_table = leaf_basis(coords, row_start, col_start)
    moments = make_moments(basis_table, vector)
    relay_level = base_level - 1
    tree_level = 0
    box_width = 2**tree_level
    rows_here = moments.shape[0]
    widened = extended(
        moments.reshape(rows_here, rows_here, column_count * 64), (("leaf", 0), ("sub", 1)), 2
    )
    window = jnp.pad(widened, ((1, 1), (1, 1), (0, 0))).reshape(
        rows_here + 6, rows_here + 6, column_count, 64
    )
    fine_local = [
        coupling_block(window, row_start // box_width, col_start // box_width, tree_level)
    ]
    moments = upward(moments)
    rows_here = moments.shape[0]
    flat_moments = moments.reshape(1, rows_here, rows_here, column_count * 64)
    gathered = lax.all_gather(flat_moments, ("leaf", "sub"), axis=0, tiled=True)
    whole_level = jnp.transpose(
        gathered.reshape(leaf_total, sub_count, rows_here, rows_here, column_count * 64),
        (0, 2, 1, 3, 4),
    ).reshape(leaf_total * rows_here, sub_count * rows_here, column_count, 64)
    coarse_local = []
    starts = []
    for tree_level in range(relay_level, top_level):
        box_width = 2**tree_level
        block_rows = max(leaf_side // box_width, 1)
        row_first = row_start // box_width
        col_first = col_start // box_width
        starts.append((row_first, col_first, block_rows))
        bordered = jnp.pad(whole_level, ((3, 3), (3, 3), (0, 0), (0, 0)))
        window = lax.dynamic_slice(
            bordered,
            (row_first, col_first, zero_index, zero_index),
            (block_rows + 6, block_rows + 6, column_count, 64),
        )
        coarse_local.append(coupling_block(window, row_first, col_first, tree_level))
        if tree_level + 1 < top_level:
            whole_level = upward(whole_level)
    summed = coarse_local[-1]
    for position in range(len(coarse_local) - 1, 0, -1):
        row_first, col_first, block_rows = starts[position - 1]
        children = downward(summed)
        row_offset = row_first - 2 * starts[position][0]
        col_offset = col_first - 2 * starts[position][1]
        summed = (
            lax.dynamic_slice(
                children,
                (row_offset, col_offset, zero_index, zero_index),
                (block_rows, block_rows, column_count, 64),
            )
            + coarse_local[position - 1]
        )
    tree_level = 1
    summed = downward(summed) + fine_local[tree_level - 1]
    return near_part + evaluate_far(basis_table, summed)


def solution(mesh):
    placed = (P(None, ("groups", "leaf"), "sub", None), P("rep", ("groups", "leaf"), "sub", None))
    return jax.shard_map(
        local,
        mesh=mesh,
        in_specs=placed,
        out_specs=P("rep", ("groups", "leaf"), "sub", None),
        check_vma=False,
    )
```

profile of v0, /device:TPU:0, one launch (start us, length us, event | category | flops | bytes accessed | tf_op | source)
XLA Modules:
  0.0 133.9 jit_solution(17107851671064558093)
XLA Ops:
  0.0 0.7 add_bitcast_fusion
  0.7 0.8 fusion.98
  1.6 0.9 multiply_add_fusion.2
  3.6 1.0 fusion.61
  4.8 4.9 %collective-permute-start.4 = (f32[2,4,256]{2,1,0:T(4,128)S(1)}, f32[2,4,256]{2,1,0:T(4,128)S(1)}, u32[]{:S(2)}, u32[]{:S(2)}) collective-permute-start(f32[2,4,256]{2,1,0:T(4,128)S(1)} %slice.872), channel_id=1, source_target_pairs={{0,4},{4,8},{8,12},{1,5},{5,9},{9,13},{2,6},{6,10},{10,14},{3,7},{... | collective-permute-start | bytes 24584 | tf_op jit(solution)/shard_map/ppermute | solution.py:20
  9.8 1.3 collective-permute-start.5
  11.1 0.6 copy.79
  11.7 3.3 %all-to-all-start = ((f32[4,4,4,256]{3,2,0,1:T(4,128)}), f32[4,4,4,256]{3,2,0,1:T(4,128)S(1)}, u32[]{:S(2)}, u32[]{:S(2)}) async-start(f32[4,4,4,256]{3,2,0,1:T(4,128)} %copy.79), calls=%async_computation | async-start | bytes 131072 | tf_op jit(solution)/shard_map/all_to_all | solution.py:227
  15.1 1.3 %all-to-all-done = f32[4,4,4,256]{3,2,0,1:T(4,128)S(1)} async-done(((f32[4,4,4,256]{3,2,0,1:T(4,128)}), f32[4,4,4,256]{3,2,0,1:T(4,128)S(1)}, u32[]{:S(2)}, u32[]{:S(2)}) %all-to-all-start) | async-done | bytes 65568 | tf_op jit(solution)/shard_map/all_to_all | solution.py:227
  16.5 2.1 %collective-permute-start = (f32[11,1,4,256]{3,0,2,1:T(8,128)S(1)}, f32[11,1,4,256]{3,0,2,1:T(8,128)S(1)}, u32[]{:S(2)}, u32[]{:S(2)}) collective-permute-start(f32[11,1,4,256]{3,0,2,1:T(8,128)S(1)} %get-tuple-element.147), channel_id=1, source_target_pairs={{0,1},{1,4},{4,5},{5,8},{8,9},{9,12},{12,13},{2,3},{3,6},{6,7},{7,... | collective-permute-start | bytes 135176 | tf_op jit(solution)/shard_map/ppermute | solution.py:20
  18.6 1.3 collective-permute-start.1
  20.4 34.0 %all_gather.3 = f32[8,2,2,256]{3,2,1,0:T(2,128)S(1)} all-gather(f32[1,2,2,256]{3,2,1,0:T(2,128)S(1)} %reshape.943), channel_id=1, replica_groups=mesh['groups'=2,'leaf'=4,'sub'=2,'rep'=2] {'leaf','sub'}, dimensions={0}, use_global_device_ids=true | all-gather | bytes 36864 | tf_op jit(solution)/shard_map/all_gather | solution.py:254
  61.6 3.7 %and_convert_fusion.15 = (f32[7]{0:T(128)S(1)}, f32[7]{0:T(128)S(1)}, f32[7]{0:T(128)S(1)}, f32[7]{0:T(128)S(1)}, f32[7]{0:T(128)S(1)}, /*index=5*/f32[7]{0:T(128)S(1)}) fusion(pred[7]{0:T(512)(128)(4,1)S(1)} %get-tuple-element.71, pred[]{:T(512)} %bitcast.99, pred[]{:T(512)} %bitcast.90, pred[]{:T(512)} %bitcast.81, pred[]{:T(512)} %bitcast.72, ...), kind=kLoop, calls=%fused_computation.619 | loop fusion | flops 84 | bytes 181 | tf_op jit(solution)/shard_map/convert_element_type | solution.py:206
  69.2 3.4 %collective-permute-start.6 = (f32[8,2,256]{2,1,0:T(2,128)S(1)}, f32[8,2,256]{2,1,0:T(2,128)S(1)}, u32[]{:S(2)}, u32[]{:S(2)}) collective-permute-start(f32[8,2,256]{2,1,0:T(2,128)S(1)} %get-tuple-element.188), channel_id=1, source_target_pairs={{0,2},{1,3},{4,6},{5,7},{8,10},{9,11},{12,14},{13,15},{16,18},{17,... | collective-permute-start | bytes 49160 | tf_op jit(solution)/shard_map/ppermute | solution.py:20
  72.6 1.5 %collective-permute-start.7 = (f32[8,2,256]{2,1,0:T(2,128)S(1)}, f32[8,2,256]{2,1,0:T(2,128)S(1)}, u32[]{:S(2)}, u32[]{:S(2)}) collective-permute-start(f32[8,2,256]{2,1,0:T(2,128)S(1)} %get-tuple-element.189), channel_id=1, source_target_pairs={{2,0},{3,1},{6,4},{7,5},{10,8},{11,9},{14,12},{15,13},{18,16},{19,... | collective-permute-start | bytes 49160 | tf_op jit(solution)/shard_map/ppermute | solution.py:21
  74.2 4.0 %collective-permute-done.7 = f32[8,2,256]{2,1,0:T(2,128)S(1)} collective-permute-done((f32[8,2,256]{2,1,0:T(2,128)S(1)}, f32[8,2,256]{2,1,0:T(2,128)S(1)}, u32[]{:S(2)}, u32[]{:S(2)}) %collective-permute-start.7) | collective-permute-done | bytes 16416 | tf_op jit(solution)/shard_map/ppermute | solution.py:21
  78.9 0.6 copy-done.25
  83.4 1.6 %collective-permute-start.2 = (f32[11,4,1,256]{3,0,2,1:T(8,128)S(1)}, f32[11,4,1,256]{3,0,2,1:T(8,128)S(1)}, u32[]{:S(2)}, u32[]{:S(2)}) collective-permute-start(f32[11,4,1,256]{3,0,2,1:T(8,128)S(1)} %get-tuple-element.96), channel_id=1, source_target_pairs={{0,2},{1,3},{4,6},{5,7},{8,10},{9,11},{12,14},{13,15},{16,18},{17,... | collective-permute-start | bytes 135176 | tf_op jit(solution)/shard_map/ppermute | solution.py:20
  85.1 1.3 collective-permute-start.3
  87.0 4.2 %collective-permute-done.3 = f32[11,4,1,256]{3,0,2,1:T(8,128)S(1)} collective-permute-done((f32[11,4,1,256]{3,0,2,1:T(8,128)S(1)}, f32[11,4,1,256]{3,0,2,1:T(8,128)S(1)}, u32[]{:S(2)}, u32[]{:S(2)}) %collective-permute-start.3) | collective-permute-done | bytes 45088 | tf_op jit(solution)/shard_map/ppermute | solution.py:21
  91.3 37.4 %while.12 = (s32[]{:T(128)}, f32[4,2,8,256]{3,2,1,0:T(8,128)S(1)}, s32[4]{0:T(128)S(1)}, f32[11,4,6,256]{3,0,2,1:T(8,128)S(1)}, s32[]{:T(128)}, /*index=5*/s32[]...) while((s32[]{:T(128)}, f32[4,2,8,256]{3,2,1,0:T(8,128)S(1)}, ...), condition=%wide.region_1.2_spmd, body=%wide.region_0.1_spmd.sunk | while | flops 125094944 | bytes 1484380 | solution.py:126
  91.3 0.7 dynamic_slice.28
  95.0 5.6 %fusion.185 = f32[4,2,8,256]{3,2,1,0:T(8,128)S(1)} fusion(f32[4,2,8,256]{3,2,1,0:T(8,128)S(1)} %get-tuple-element.365, s32[]{:T(128)} %get-tuple-element.364, f32[2,256]{1,0:T(2,128)S(1)} %get-tuple-element.331, f32[2,9,256]{2,1,0:T(8,128)S(1)} %copy.231, f32[2,256]{1,0:T(2,128)S(1)} %get-tuple-element.347, f32[2,9,256]{2,1,0:T(8,128)S(1)} %copy.232, ...), kind=kOutput, calls=%fused_computation.21.clone.1 | convolution fusion | flops 125079552 | bytes 415748 | tf_op jit(solution)/shard_map/while/body/eval_jaxpr/vmap(cnb,nba->ca)/dot_general | solution.py:93
  100.7 0.7 dynamic_slice.28
  104.4 5.6 %fusion.185 = f32[4,2,8,256]{3,2,1,0:T(8,128)S(1)} fusion(f32[4,2,8,256]{3,2,1,0:T(8,128)S(1)} %get-tuple-element.365, s32[]{:T(128)} %get-tuple-element.364, f32[2,256]{1,0:T(2,128)S(1)} %get-tuple-element.331, f32[2,9,256]{2,1,0:T(8,128)S(1)} %copy.231, f32[2,256]{1,0:T(2,128)S(1)} %get-tuple-element.347, f32[2,9,256]{2,1,0:T(8,128)S(1)} %copy.232, ...), kind=kOutput, calls=%fused_computation.21.clone.1 | convolution fusion | flops 125079552 | bytes 415748 | tf_op jit(solution)/shard_map/while/body/eval_jaxpr/vmap(cnb,nba->ca)/dot_general | solution.py:93
  110.0 0.7 dynamic_slice.28
  113.7 5.6 %fusion.185 = f32[4,2,8,256]{3,2,1,0:T(8,128)S(1)} fusion(f32[4,2,8,256]{3,2,1,0:T(8,128)S(1)} %get-tuple-element.365, s32[]{:T(128)} %get-tuple-element.364, f32[2,256]{1,0:T(2,128)S(1)} %get-tuple-element.331, f32[2,9,256]{2,1,0:T(8,128)S(1)} %copy.231, f32[2,256]{1,0:T(2,128)S(1)} %get-tuple-element.347, f32[2,9,256]{2,1,0:T(8,128)S(1)} %copy.232, ...), kind=kOutput, calls=%fused_computation.21.clone.1 | convolution fusion | flops 125079552 | bytes 415748 | tf_op jit(solution)/shard_map/while/body/eval_jaxpr/vmap(cnb,nba->ca)/dot_general | solution.py:93
  119.4 0.7 dynamic_slice.28
  123.1 5.6 %fusion.185 = f32[4,2,8,256]{3,2,1,0:T(8,128)S(1)} fusion(f32[4,2,8,256]{3,2,1,0:T(8,128)S(1)} %get-tuple-element.365, s32[]{:T(128)} %get-tuple-element.364, f32[2,256]{1,0:T(2,128)S(1)} %get-tuple-element.331, f32[2,9,256]{2,1,0:T(8,128)S(1)} %copy.231, f32[2,256]{1,0:T(2,128)S(1)} %get-tuple-element.347, f32[2,9,256]{2,1,0:T(8,128)S(1)} %copy.232, ...), kind=kOutput, calls=%fused_computation.21.clone.1 | convolution fusion | flops 125079552 | bytes 415748 | tf_op jit(solution)/shard_map/while/body/eval_jaxpr/vmap(cnb,nba->ca)/dot_general | solution.py:93
  128.8 3.8 %all_to_all.36 = f32[8,2,4,256]{3,2,1,0:T(4,128)S(1)} all-to-all(f32[8,2,4,256]{3,2,1,0:T(4,128)S(1)} %bitcast.825), channel_id=1, replica_groups=mesh['groups'=2,'leaf'=4,'sub'=2,'rep'=2] {'rep'}, dimensions={0} | all-to-all | bytes 131072 | tf_op jit(solution)/shard_map/all_to_all | solution.py:233
  132.6 0.6 fusion.33
  133.2 0.6 copy.87
  (278 shorter events, 18.5 us)
Async XLA Ops:
  3.6 11.4 %copy-start.16 = (f32[3,4,4,256]{3,2,1,0:T(4,128)S(1)}, f32[3,4,4,256]{3,2,1,0:T(4,128)}, u32[]{:S(2)}) copy-start(f32[3,4,4,256]{3,2,1,0:T(4,128)} %param.20) | copy-start | bytes 147460
  3.6 16.4 %copy-start.18 = (f32[2,2,64,64,1,1]{3,2,1,4,5,0:T(8,128)S(1)}, f32[2,2,64,64,1,1]{3,2,1,4,5,0:T(8,128)}, u32[]{:S(2)}) copy-start(f32[2,2,64,64,1,1]{3,2,1,4,5,0:T(8,128)} %constant.347) | copy-start | bytes 196612
  4.8 64.4 %collective-permute-start.4 = (f32[2,4,256]{2,1,0:T(4,128)S(1)}, f32[2,4,256]{2,1,0:T(4,128)S(1)}, u32[]{:S(2)}, u32[]{:S(2)}) collective-permute-start(f32[2,4,256]{2,1,0:T(4,128)S(1)} %slice.872), channel_id=1, source_target_pairs={{0,4},{4,8},{8,12},{1,5},{5,9},{9,13},{2,6},{6,10},{10,14},{3,7},{... | collective-permute-start | bytes 24584 | tf_op jit(solution)/shard_map/ppermute | solution.py:20
  9.8 59.4 %collective-permute-start.5 = (f32[2,4,256]{2,1,0:T(4,128)S(1)}, f32[2,4,256]{2,1,0:T(4,128)S(1)}, u32[]{:S(2)}, u32[]{:S(2)}) collective-permute-start(f32[2,4,256]{2,1,0:T(4,128)S(1)} %slice.874), channel_id=1, source_target_pairs={{4,0},{8,4},{12,8},{5,1},{9,5},{13,9},{6,2},{10,6},{14,10},{7,3},{... | collective-permute-start | bytes 24584 | tf_op jit(solution)/shard_map/ppermute | solution.py:21
  11.7 4.7 %all-to-all-start = ((f32[4,4,4,256]{3,2,0,1:T(4,128)}), f32[4,4,4,256]{3,2,0,1:T(4,128)S(1)}, u32[]{:S(2)}, u32[]{:S(2)}) async-start(f32[4,4,4,256]{3,2,0,1:T(4,128)} %copy.79), calls=%async_computation | async-start | bytes 131072 | tf_op jit(solution)/shard_map/all_to_all | solution.py:227
  16.5 66.9 %collective-permute-start = (f32[11,1,4,256]{3,0,2,1:T(8,128)S(1)}, f32[11,1,4,256]{3,0,2,1:T(8,128)S(1)}, u32[]{:S(2)}, u32[]{:S(2)}) collective-permute-start(f32[11,1,4,256]{3,0,2,1:T(8,128)S(1)} %get-tuple-element.147), channel_id=1, source_target_pairs={{0,1},{1,4},{4,5},{5,8},{8,9},{9,12},{12,13},{2,3},{3,6},{6,7},{7,... | collective-permute-start | bytes 135176 | tf_op jit(solution)/shard_map/ppermute | solution.py:20
  18.6 64.9 %collective-permute-start.1 = (f32[11,1,4,256]{3,0,2,1:T(8,128)S(1)}, f32[11,1,4,256]{3,0,2,1:T(8,128)S(1)}, u32[]{:S(2)}, u32[]{:S(2)}) collective-permute-start(f32[11,1,4,256]{3,0,2,1:T(8,128)S(1)} %get-tuple-element.148), channel_id=1, source_target_pairs={{1,0},{4,1},{5,4},{8,5},{9,8},{12,9},{13,12},{3,2},{6,3},{7,6},{10... | collective-permute-start | bytes 135176 | tf_op jit(solution)/shard_map/ppermute | solution.py:21
  54.9 1.8 %copy-start = (f32[2,2,64,64,1,1]{3,2,1,0,5,4:T(8,128)S(1)}, f32[2,2,64,64,1,1]{3,2,1,0,5,4:T(8,128)}, u32[]{:S(2)}) copy-start(f32[2,2,64,64,1,1]{3,2,1,0,5,4:T(8,128)} %constant.348) | copy-start | bytes 196612
  55.4 3.1 %copy-start.8 = (f32[7,64,64,1,1]{2,1,3,4,0:T(8,128)S(1)}, f32[7,64,64,1,1]{2,1,3,4,0:T(8,128)}, u32[]{:S(2)}) copy-start(f32[7,64,64,1,1]{2,1,3,4,0:T(8,128)} %constant.349) | copy-start | bytes 344068
  55.6 3.4 %copy-start.7 = (f32[7,64,64,1,1]{2,1,3,4,0:T(8,128)S(1)}, f32[7,64,64,1,1]{2,1,3,4,0:T(8,128)}, u32[]{:S(2)}) copy-start(f32[7,64,64,1,1]{2,1,3,4,0:T(8,128)} %constant.350) | copy-start | bytes 344068
  55.7 3.7 %copy-start.6 = (f32[7,64,64,1,1]{2,1,3,4,0:T(8,128)S(1)}, f32[7,64,64,1,1]{2,1,3,4,0:T(8,128)}, u32[]{:S(2)}) copy-start(f32[7,64,64,1,1]{2,1,3,4,0:T(8,128)} %constant.351) | copy-start | bytes 344068
  55.9 4.0 %copy-start.5 = (f32[7,64,64,1,1]{2,1,3,4,0:T(8,128)S(1)}, f32[7,64,64,1,1]{2,1,3,4,0:T(8,128)}, u32[]{:S(2)}) copy-start(f32[7,64,64,1,1]{2,1,3,4,0:T(8,128)} %constant.352) | copy-start | bytes 344068
  56.7 3.7 %copy-start.4 = (f32[7,64,64,1,1]{2,1,3,4,0:T(8,128)S(1)}, f32[7,64,64,1,1]{2,1,3,4,0:T(8,128)}, u32[]{:S(2)}) copy-start(f32[7,64,64,1,1]{2,1,3,4,0:T(8,128)} %constant.353) | copy-start | bytes 344068
  57.2 3.5 %copy-start.3 = (f32[7,64,64,1,1]{2,1,3,4,0:T(8,128)S(1)}, f32[7,64,64,1,1]{2,1,3,4,0:T(8,128)}, u32[]{:S(2)}) copy-start(f32[7,64,64,1,1]{2,1,3,4,0:T(8,128)} %constant.354) | copy-start | bytes 344068
  57.6 3.6 %copy-start.2 = (f32[7,64,64,1,1]{2,1,3,4,0:T(8,128)S(1)}, f32[7,64,64,1,1]{2,1,3,4,0:T(8,128)}, u32[]{:S(2)}) copy-start(f32[7,64,64,1,1]{2,1,3,4,0:T(8,128)} %constant.355) | copy-start | bytes 344068
  58.5 6.8 %copy-start.15 = (f32[7,64,64]{2,1,0:T(8,128)S(1)}, f32[7,64,64]{2,1,0:T(8,128)}, u32[]{:S(2)}) copy-start(f32[7,64,64]{2,1,0:T(8,128)} %constant.306) | copy-start | bytes 344068
  59.0 6.7 %copy-start.14 = (f32[7,64,64]{2,1,0:T(8,128)S(1)}, f32[7,64,64]{2,1,0:T(8,128)}, u32[]{:S(2)}) copy-start(f32[7,64,64]{2,1,0:T(8,128)} %constant.308) | copy-start | bytes 344068
  59.4 6.7 %copy-start.13 = (f32[7,64,64]{2,1,0:T(8,128)S(1)}, f32[7,64,64]{2,1,0:T(8,128)}, u32[]{:S(2)}) copy-start(f32[7,64,64]{2,1,0:T(8,128)} %constant.310) | copy-start | bytes 344068
  59.9 6.6 %copy-start.12 = (f32[7,64,64]{2,1,0:T(8,128)S(1)}, f32[7,64,64]{2,1,0:T(8,128)}, u32[]{:S(2)}) copy-start(f32[7,64,64]{2,1,0:T(8,128)} %constant.312) | copy-start | bytes 344068
  60.3 6.6 %copy-start.11 = (f32[7,64,64]{2,1,0:T(8,128)S(1)}, f32[7,64,64]{2,1,0:T(8,128)}, u32[]{:S(2)}) copy-start(f32[7,64,64]{2,1,0:T(8,128)} %constant.314) | copy-start | bytes 344068
  60.3 6.9 %copy-start.10 = (f32[7,64,64]{2,1,0:T(8,128)S(1)}, f32[7,64,64]{2,1,0:T(8,128)}, u32[]{:S(2)}) copy-start(f32[7,64,64]{2,1,0:T(8,128)} %constant.316) | copy-start | bytes 344068
  60.8 6.9 %copy-start.9 = (f32[7,64,64]{2,1,0:T(8,128)S(1)}, f32[7,64,64]{2,1,0:T(8,128)}, u32[]{:S(2)}) copy-start(f32[7,64,64]{2,1,0:T(8,128)} %constant.318) | copy-start | bytes 344068
  61.2 6.8 %copy-start.17 = (f32[2,2,64,64]{3,2,1,0:T(8,128)S(1)}, f32[2,2,64,64]{3,2,1,0:T(8,128)}, u32[]{:S(2)}) copy-start(f32[2,2,64,64]{3,2,1,0:T(8,128)} %constant.294.clone) | copy-start | bytes 196612
  69.2 5.0 %collective-permute-start.6 = (f32[8,2,256]{2,1,0:T(2,128)S(1)}, f32[8,2,256]{2,1,0:T(2,128)S(1)}, u32[]{:S(2)}, u32[]{:S(2)}) collective-permute-start(f32[8,2,256]{2,1,0:T(2,128)S(1)} %get-tuple-element.188), channel_id=1, source_target_pairs={{0,2},{1,3},{4,6},{5,7},{8,10},{9,11},{12,14},{13,15},{16,18},{17,... | collective-permute-start | bytes 49160 | tf_op jit(solution)/shard_map/ppermute | solution.py:20
  72.6 5.6 %collective-permute-start.7 = (f32[8,2,256]{2,1,0:T(2,128)S(1)}, f32[8,2,256]{2,1,0:T(2,128)S(1)}, u32[]{:S(2)}, u32[]{:S(2)}) collective-permute-start(f32[8,2,256]{2,1,0:T(2,128)S(1)} %get-tuple-element.189), channel_id=1, source_target_pairs={{2,0},{3,1},{6,4},{7,5},{10,8},{11,9},{14,12},{15,13},{18,16},{19,... | collective-permute-start | bytes 49160 | tf_op jit(solution)/shard_map/ppermute | solution.py:21
  78.7 2.1 %copy-start.23 = (f32[7,64,64,1,1]{2,1,3,4,0:T(8,128)S(1)}, f32[7,64,64,1,1]{2,1,3,4,0:T(8,128)}, u32[]{:S(2)}) copy-start(f32[7,64,64,1,1]{2,1,3,4,0:T(8,128)} %constant.358) | copy-start | bytes 344068
  78.8 2.7 %copy-start.22 = (f32[7,64,64,1,1]{2,1,3,4,0:T(8,128)S(1)}, f32[7,64,64,1,1]{2,1,3,4,0:T(8,128)}, u32[]{:S(2)}) copy-start(f32[7,64,64,1,1]{2,1,3,4,0:T(8,128)} %constant.359) | copy-start | bytes 344068
  79.5 2.6 %copy-start.21 = (f32[7,64,64,1,1]{2,1,3,4,0:T(8,128)S(1)}, f32[7,64,64,1,1]{2,1,3,4,0:T(8,128)}, u32[]{:S(2)}) copy-start(f32[7,64,64,1,1]{2,1,3,4,0:T(8,128)} %constant.360) | copy-start | bytes 344068
  80.2 2.6 %copy-start.20 = (f32[7,64,64,1,1]{2,1,3,4,0:T(8,128)S(1)}, f32[7,64,64,1,1]{2,1,3,4,0:T(8,128)}, u32[]{:S(2)}) copy-start(f32[7,64,64,1,1]{2,1,3,4,0:T(8,128)} %constant.361) | copy-start | bytes 344068
  81.5 4.9 %copy-start.19 = (f32[7,64,64,1,1]{2,1,3,4,0:T(8,128)S(1)}, f32[7,64,64,1,1]{2,1,3,4,0:T(8,128)}, u32[]{:S(2)}) copy-start(f32[7,64,64,1,1]{2,1,3,4,0:T(8,128)} %constant.362) | copy-start | bytes 344068
  83.4 3.6 %collective-permute-start.2 = (f32[11,4,1,256]{3,0,2,1:T(8,128)S(1)}, f32[11,4,1,256]{3,0,2,1:T(8,128)S(1)}, u32[]{:S(2)}, u32[]{:S(2)}) collective-permute-start(f32[11,4,1,256]{3,0,2,1:T(8,128)S(1)} %get-tuple-element.96), channel_id=1, source_target_pairs={{0,2},{1,3},{4,6},{5,7},{8,10},{9,11},{12,14},{13,15},{16,18},{17,... | collective-permute-start | bytes 135176 | tf_op jit(solution)/shard_map/ppermute | solution.py:20
  85.1 6.2 %collective-permute-start.3 = (f32[11,4,1,256]{3,0,2,1:T(8,128)S(1)}, f32[11,4,1,256]{3,0,2,1:T(8,128)S(1)}, u32[]{:S(2)}, u32[]{:S(2)}) collective-permute-start(f32[11,4,1,256]{3,0,2,1:T(8,128)S(1)} %get-tuple-element.97), channel_id=1, source_target_pairs={{2,0},{3,1},{6,4},{7,5},{10,8},{11,9},{14,12},{15,13},{18,16},{19,... | collective-permute-start | bytes 135176 | tf_op jit(solution)/shard_map/ppermute | solution.py:21
  (3 other events, 3.3 us)
where the time goes:
time: 135 us; the launch traced here: 134 us
  blocking collectives  37.8 us (28%)
  matrix products  35.3 us (26%)
  starting transfers between devices  20.7 us (15%)
  loops' own time  11.1 us (8%)
  local copies, waits for them, and re-layouts  10.3 us (8%)
  waiting for transfers between devices  9.59 us (7%)
  other arithmetic  7.78 us (6%)
    all_gather x1, blocking collectives, local(): gathered = lax.all_gather(flat_moments, ('leaf', 'sub'), axis=0, tiled=True)  34 us
    dot_general x4, matrix products, near_leaf(): return jnp.einsum('cnb,nba->ca', source[3:], kernel, precision=HIGHEST)  22.6 us
    ppermute x4, starting transfers between devices, extended(): before = lax.ppermute(last, axis, up)  12 us
    another operation x1, loops' own time, near_block(): lax.map(per_pair, jnp.arange(rows_here * pair_rows, dtype=jnp.int32))  11.1 us
    dot_general x21, matrix products, coupling_block(): jnp.einsum('vxycs,vrs->xycr', slab * weight[:, :, :, None, None], table[r...  9.66 us
    ppermute x4, waiting for transfers between devices, extended(): after = lax.ppermute(leading, axis, down)  8.24 us
    ppermute x4, starting transfers between devices, extended(): after = lax.ppermute(leading, axis, down)  5.34 us
    convert_element_type x4, other arithmetic, coupling_block(): (row_ok[row_shift][None, :, None] & col_ok[:, None, :]).astype(jnp.float32)  4.46 us
  transfers between devices with their start and end apart: 9, of which 3 were waited for; matrix products, arithmetic and copies ran while one was open for 15% of the time, Pallas kernels for 0%

commit v1 on v0

v1 whole, which is shorter than its diff:
```python
import functools

import jax
import jax.numpy as jnp
import numpy as np
from jax import lax
from jax.experimental import pallas as pl
from jax.experimental.pallas import tpu as pltpu
from jax.sharding import PartitionSpec as P

QUAD_WEIGHT = 1.0 / 64.0
SMOOTHING = 0.01
CHEB_NODES = np.cos((2.0 * np.arange(4) + 1.0) * np.pi / 8.0)
SIDE = 4
F32 = jnp.float32
BF16 = jnp.bfloat16
MESH = pl.DeviceIdType.MESH
DIRECTIONS = [(-1, 0), (1, 0), (0, -1), (0, 1), (-1, -1), (-1, 1), (1, -1), (1, 1)]


def poly_values(points):
    second = 2.0 * points * points - 1.0
    third = 2.0 * points * second - points
    return (points, second, third)


def cheb_numpy(values):
    nodes_one, nodes_two, nodes_three = poly_values(CHEB_NODES)
    first, second, third = poly_values(values)
    return 0.25 + 0.5 * (
        first[..., None] * nodes_one
        + second[..., None] * nodes_two
        + third[..., None] * nodes_three
    )


def transfer_table():
    halves = [cheb_numpy((CHEB_NODES + 2.0 * side_bit - 1.0) / 2.0) for side_bit in range(2)]
    same_node = np.eye(4)
    blocks = [
        [
            (
                halves[row_bit][:, None, None, :, None, None]
                * halves[col_bit][None, :, None, None, :, None]
                * same_node[None, None, :, None, None, :]
            ).reshape(64, 64)
            for col_bit in range(2)
        ]
        for row_bit in range(2)
    ]
    return np.array(blocks)


def couple_table(tree_level):
    box_width = 2.0**tree_level
    across = 0.5 * box_width * CHEB_NODES
    height = 0.5 + 0.5 * CHEB_NODES
    target = np.stack(np.meshgrid(across, across, height, indexing="ij"), -1).reshape(64, 3)
    table_rows = []
    for row_shift in range(-3, 4):
        table_line = []
        for col_shift in range(-3, 4):
            source = target + np.array([row_shift * box_width, col_shift * box_width, 0.0])
            spacing = target[:, None, :] - source[None, :, :]
            values = QUAD_WEIGHT / np.sqrt(np.sum(spacing * spacing, -1) + SMOOTHING)
            far_flag = float(max(abs(row_shift), abs(col_shift)) >= 2)
            table_line.append(values * far_flag)
        table_rows.append(table_line)
    return np.array(table_rows)


def parent_couplings(tree_level):
    table = couple_table(tree_level).astype(np.float32)
    full = np.zeros((3, 3, 2, 2, 64, 2, 2, 64), np.float32)
    for pi in range(3):
        for pj in range(3):
            for sd in range(2):
                for se in range(2):
                    for td in range(2):
                        for te in range(2):
                            u = 2 * (pi - 1) + sd - td
                            v = 2 * (pj - 1) + se - te
                            full[pi, pj, sd, se, :, td, te, :] = table[u + 3, v + 3].T
    return full.reshape(2304, 256)


def halves_numpy(values):
    values = np.asarray(values, np.float32)
    high = values.astype(BF16)
    low = (values - high.astype(np.float32)).astype(BF16)
    return high, low


def halves(values):
    high = values.astype(BF16).astype(F32)
    return high, values - high


def rows_of_halves(values):
    high, low = halves(values)
    return jnp.concatenate([high, low], 0).astype(BF16)


def mm(left, right):
    return jnp.dot(left, right, preferred_element_type=F32)


def mm_nt(left, right):
    return lax.dot_general(left, right, (((1,), (1,)), ((), ())), preferred_element_type=F32)


def mm_split(values, high, low):
    rows = values.shape[0]
    stacked = rows_of_halves(values)
    first = mm(stacked, high)
    second = mm(stacked[:rows], low)
    return first[:rows] + first[rows:] + second


def wide_node(points, coefs):
    first, second, third = poly_values(points)
    return 0.25 + 0.5 * (first * coefs[0] + second * coefs[1] + third * coefs[2])


def body(
    leaf_total,
    sub_total,
    coarse_levels,
    coords_ref,
    vector_ref,
    node_ref,
    up_ref,
    down_ref,
    fine_hbm,
    coarse_hbm,
    out_ref,
    pack,
    basis,
    flipped,
    near,
    mom,
    gathered,
    level_mom,
    fine_w,
    coarse_w,
    weight_sem,
    coarse_sem,
    pack_send,
    pack_recv,
    mom_send,
    mom_recv,
    all_send,
    all_recv,
):
    leaf_at = lax.axis_index("leaf")
    sub_at = lax.axis_index("sub")
    me = leaf_at * sub_total + sub_at
    count = leaf_total * sub_total

    def peer(step):
        other = lax.rem(me + step, count)
        return other, {"leaf": other // sub_total, "sub": lax.rem(other, sub_total)}

    fine_copy = pltpu.make_async_copy(fine_hbm, fine_w, weight_sem)
    fine_copy.start()
    coarse_copies = []
    for pos in range(coarse_levels):
        row_bit = lax.rem(leaf_at // 2**pos, 2)
        col_bit = lax.rem(sub_at // 2**pos, 2)
        coarse_copies.append(
            pltpu.make_async_copy(
                coarse_hbm.at[pos, 2 * row_bit + col_bit], coarse_w.at[pos], coarse_sem.at[pos]
            )
        )
        coarse_copies[-1].start()

    empty = jnp.zeros((8, 256), F32)
    for k in range(SIDE + 2):
        pack[0, k] = empty
        pack[SIDE + 1, k] = empty
        pack[k, 0] = empty
        pack[k, SIDE + 1] = empty
    for k in range(4):
        mom[0, k] = empty
        mom[3, k] = empty
        mom[k, 0] = empty
        mom[k, 3] = empty

    barrier = pltpu.get_barrier_semaphore()

    def greet(step, carry):
        _, where = peer(step)
        pl.semaphore_signal(barrier, inc=1, device_id=where, device_id_type=MESH)
        return carry

    lax.fori_loop(1, count, greet, 0)

    row_start = (leaf_at * SIDE).astype(F32) + 0.5
    col_start = (sub_at * SIDE).astype(F32) + 0.5
    for i in range(SIDE):
        for j in range(SIDE):
            pack[i + 1, j + 1, 0:1] = coords_ref[0, i, j : j + 1] - (row_start + float(i))
            pack[i + 1, j + 1, 1:2] = coords_ref[1, i, j : j + 1] - (col_start + float(j))
            pack[i + 1, j + 1, 2:3] = coords_ref[2, i, j : j + 1] - 0.5
            pack[i + 1, j + 1, 3:4] = jnp.zeros((1, 256), F32)
            for c in range(4):
                pack[i + 1, j + 1, 4 + c : 5 + c] = vector_ref[c, i, j : j + 1]

    pl.semaphore_wait(barrier, count - 1)

    def edge(inner, shift):
        if shift == 0:
            return pl.ds(1, inner), pl.ds(1, inner)
        if shift < 0:
            return pl.ds(1, 1), pl.ds(inner + 1, 1)
        return pl.ds(inner, 1), pl.ds(0, 1)

    def halo(ref, inner, send, recv):
        copies = []
        for k, (di, dj) in enumerate(DIRECTIONS):
            src_i, dst_i = edge(inner, di)
            src_j, dst_j = edge(inner, dj)
            to_ok = (leaf_at + di >= 0) & (leaf_at + di < leaf_total)
            to_ok = to_ok & (sub_at + dj >= 0) & (sub_at + dj < sub_total)
            from_ok = (leaf_at - di >= 0) & (leaf_at - di < leaf_total)
            from_ok = from_ok & (sub_at - dj >= 0) & (sub_at - dj < sub_total)
            copy = pltpu.make_async_remote_copy(
                src_ref=ref.at[src_i, src_j],
                dst_ref=ref.at[dst_i, dst_j],
                send_sem=send.at[k],
                recv_sem=recv.at[k],
                device_id={"leaf": leaf_at + di, "sub": sub_at + dj},
                device_id_type=MESH,
            )
            copies.append((copy, to_ok, from_ok))
        for copy, to_ok, _ in copies:
            pl.when(to_ok)(copy.start)
        return copies

    def halo_wait(copies):
        for copy, to_ok, from_ok in copies:
            pl.when(to_ok)(copy.wait_send)
            pl.when(from_ok)(copy.wait_recv)

    pack_copies = halo(pack, SIDE, pack_send, pack_recv)

    nodes = np.array(poly_values(CHEB_NODES))
    y_coefs = [node_ref[n] for n in range(3)]
    z_coefs = [node_ref[3 + n] for n in range(3)]
    row_id = lax.broadcasted_iota(jnp.int32, (8, 256), 0)
    for i in range(SIDE):
        for j in range(SIDE):
            box = pack[i + 1, j + 1]
            y_part = wide_node(2.0 * box[1:2], y_coefs)
            z_part = wide_node(2.0 * box[2:3], z_coefs)
            yz_part = y_part * z_part
            x_first = poly_values(2.0 * box[0:1])
            planes = []
            for k in range(4):
                weight = 0.25 + 0.5 * sum(x_first[n] * float(nodes[n, k]) for n in range(3))
                planes.append(yz_part * weight)
            wide = rows_of_halves(jnp.concatenate(planes, 0))
            basis[i * SIDE + j] = wide
            vec = box[4:8]
            v_high, v_low = halves(vec)
            both = jnp.concatenate([v_high, v_low, jnp.zeros((8, 256), F32)], 0).astype(BF16)
            got = mm_nt(both, wide)
            piece = got[0:4, 0:64] + got[4:8, 0:64] + got[0:4, 64:128]
            at = 64 * (2 * (i % 2) + j % 2)
            mom[1 + i // 2, 1 + j // 2, 0:4, at : at + 64] = piece
            mom[1 + i // 2, 1 + j // 2, 4:8, at : at + 64] = jnp.zeros((4, 64), F32)
    mom_copies = halo(mom, 2, mom_send, mom_recv)
    parents = jnp.concatenate([mom[1, 1], mom[1, 2], mom[2, 1], mom[2, 2]], 0)
    raised = mm_split(parents, up_ref[0], up_ref[1])
    gathered[me] = jnp.concatenate([raised[8 * k : 8 * k + 8] for k in range(4)], 1)

    def spread_copy(step, own_slot):
        other, where = peer(step)
        slot = me if own_slot else other
        return pltpu.make_async_remote_copy(
            src_ref=gathered.at[me],
            dst_ref=gathered.at[slot],
            send_sem=all_send.at[other],
            recv_sem=all_recv.at[slot],
            device_id=where,
            device_id_type=MESH,
        )

    def spread(step, carry):
        spread_copy(step, True).start()
        return carry

    lax.fori_loop(1, count, spread, 0)

    ones = jnp.ones((8, 256), F32)

    def parts_of(tile):
        first = tile.astype(BF16).astype(F32)
        rest = tile - first
        second = rest.astype(BF16).astype(F32)
        return first, second, rest - second

    def squares(tile):
        sq = tile * tile
        return sq[0:1] + sq[1:2] + sq[2:3]

    for i in range(SIDE):
        for j in range(SIDE):
            box = pack[i + 1, j + 1]
            first, second, third = parts_of(jnp.where(row_id < 3, box, 0.0))
            n_first, n_second, n_third = parts_of(squares(box))
            groups = []
            for piece, norm in (
                (first, n_first),
                (first, n_second),
                (first, n_third),
            ):
                tile = jnp.where(row_id == 3, ones, -2.0 * piece)
                groups.append(jnp.where(row_id == 4, norm, tile))
            groups += [-2.0 * second, -2.0 * second, -2.0 * third]
            groups.append(jnp.zeros((80, 256), F32))
            flipped[i * SIDE + j] = jnp.concatenate(groups, 0).T.astype(BF16)

    halo_wait(pack_copies)

    def near_box(box_at, carry):
        i = box_at // SIDE
        j = lax.rem(box_at, SIDE)
        target = flipped[box_at][:, :48]
        total = jnp.zeros((256, 16), F32)
        for di in range(3):
            for dj in range(3):
                box = pack[i + di, j + dj]
                moved = jnp.where(row_id == 0, box + float(di - 1), box)
                moved = jnp.where(row_id == 1, box + float(dj - 1), moved)
                norm = squares(moved) + SMOOTHING
                tile = jnp.where(row_id == 3, norm, jnp.where(row_id < 3, moved, 0.0))
                first, second, third = parts_of(tile)
                stacked = [
                    jnp.where(row_id == 4, ones, first),
                    jnp.where(row_id == 4, ones, second),
                    jnp.where(row_id == 4, ones, third),
                    first,
                    second,
                    first,
                ]
                source = jnp.concatenate(stacked, 0).astype(BF16)
                v_high, v_low = halves(box[4:8])
                vec = jnp.concatenate([v_high, v_low, jnp.zeros((8, 256), F32)], 0).astype(BF16)
                kern = lax.rsqrt(mm(target, source))
                high = kern.astype(BF16)
                low = (kern - high.astype(F32)).astype(BF16)
                total = total + mm_nt(high, vec) + mm_nt(low, vec)
        wide = jnp.concatenate([total, jnp.zeros((256, 112), F32)], 1).T
        near[box_at] = QUAD_WEIGHT * (wide[0:4] + wide[4:8])
        return carry

    lax.fori_loop(0, SIDE * SIDE, near_box, 0)

    def spread_wait(step, carry):
        spread_copy(step, True).wait_send()
        spread_copy(step, False).wait_recv()
        return carry

    lax.fori_loop(1, count, spread_wait, 0)

    def padded_read(row, col):
        row_ok = (row >= 0) & (row < leaf_total)
        col_ok = (col >= 0) & (col < sub_total)
        at = jnp.clip(row, 0, leaf_total - 1) * sub_total + jnp.clip(col, 0, sub_total - 1)
        return jnp.where(row_ok & col_ok, gathered[at], 0.0)

    for copy in coarse_copies:
        copy.wait()
    current = gathered[...].reshape(count * 8, 256)
    rows_here, cols_here = leaf_total, sub_total
    coarse_local = []
    for pos in range(coarse_levels):
        raised = mm_split(current, up_ref[0], up_ref[1])
        p_rows, p_cols = rows_here // 2, cols_here // 2
        for a in range(p_rows + 2):
            for b in range(p_cols + 2):
                if a in (0, p_rows + 1) or b in (0, p_cols + 1):
                    level_mom[pos, a, b] = empty
        tiles = []
        for a in range(p_rows):
            for b in range(p_cols):
                kids = []
                for d in range(2):
                    for e in range(2):
                        at = 8 * ((2 * a + d) * cols_here + 2 * b + e)
                        kids.append(raised[at : at + 8])
                tile = jnp.concatenate(kids, 1)
                level_mom[pos, a + 1, b + 1] = tile
                tiles.append(tile)
        pi = leaf_at // 2 ** (pos + 1)
        pj = sub_at // 2 ** (pos + 1)
        window = jnp.concatenate(
            [level_mom[pos, pi + a, pj + b] for a in range(3) for b in range(3)], 1
        )
        got = mm(rows_of_halves(window), coarse_w[pos])
        coarse_local.append(got[0:8, 0:64] + got[8:16, 0:64] + got[0:8, 64:128])
        current = jnp.concatenate(tiles, 0)
        rows_here, cols_here = p_rows, p_cols

    summed = coarse_local[-1]
    for pos in range(coarse_levels - 1, 0, -1):
        children = mm_split(summed, down_ref[0], down_ref[1])
        row_bit = lax.rem(leaf_at // 2 ** (pos - 1), 2)
        col_bit = lax.rem(sub_at // 2 ** (pos - 1), 2)
        child = 2 * row_bit + col_bit
        summed = coarse_local[pos - 1]
        for k in range(4):
            summed = summed + jnp.where(child == k, children[:, 64 * k : 64 * k + 64], 0.0)

    halo_wait(mom_copies)
    fine_copy.wait()
    window = jnp.concatenate(
        [padded_read(leaf_at + a, sub_at + b) for a in (-1, 0, 1) for b in (-1, 0, 1)], 1
    )
    level_one = mm_split(summed, down_ref[0], down_ref[1]) + mm_split(
        window, fine_w[1, 0], fine_w[1, 1]
    )
    stacked = jnp.concatenate([level_one[:, 64 * k : 64 * k + 64] for k in range(4)], 0)
    window = jnp.concatenate(
        [
            jnp.concatenate([mom[a + di, b + dj] for a in range(2) for b in range(2)], 0)
            for di in range(3)
            for dj in range(3)
        ],
        1,
    )
    level_zero = mm_split(stacked, down_ref[0], down_ref[1]) + mm_split(
        window, fine_w[0, 0], fine_w[0, 1]
    )
    for i in range(SIDE):
        for j in range(SIDE):
            row = 8 * (2 * (i // 2) + j // 2)
            at = 64 * (2 * (i % 2) + j % 2)
            coef = level_zero[row : row + 8, at : at + 64]
            high, low = halves(coef)
            wide = basis[i * SIDE + j]
            left = jnp.concatenate([high, low], 0).astype(BF16)
            got = mm(left, wide[:64])
            got_low = mm(left, wide[64:])
            result = near[i * SIDE + j] + got[0:4] + got[8:12] + got_low[0:4]
            for c in range(4):
                out_ref[c, i, j : j + 1] = result[c : c + 1]


def local(coords, vector):
    leaf_total = lax.axis_size("leaf")
    sub_total = lax.axis_size("sub")
    count = leaf_total * sub_total
    top_level = (SIDE * sub_total).bit_length() - 1
    coarse_levels = top_level - 2

    nodes = np.array(poly_values(CHEB_NODES))
    index = np.arange(16)
    node_table = np.concatenate([nodes[:, index // 4], nodes[:, index % 4]], 0)
    node_table = np.repeat(node_table[:, :, None], 256, 2).astype(np.float32)
    table = transfer_table()
    up = np.stack(halves_numpy(table.reshape(256, 64)))
    down = np.stack(halves_numpy(table.reshape(256, 64).T))
    fine = np.stack([np.stack(halves_numpy(parent_couplings(level))) for level in range(2)])
    coarse = []
    for level in range(2, top_level):
        high, low = halves_numpy(parent_couplings(level))
        high = high.reshape(2304, 4, 64).transpose(1, 0, 2)
        low = low.reshape(2304, 4, 64).transpose(1, 0, 2)
        coarse.append(np.concatenate([high, low], 2))
    coarse = np.stack(coarse)

    vmem = pl.BlockSpec(memory_space=pltpu.VMEM)
    hbm = pl.BlockSpec(memory_space=pl.ANY)
    dma = pltpu.SemaphoreType.DMA
    return pl.pallas_call(
        functools.partial(body, leaf_total, sub_total, coarse_levels),
        out_shape=jax.ShapeDtypeStruct(vector.shape, F32),
        in_specs=[vmem, vmem, vmem, vmem, vmem, hbm, hbm],
        out_specs=vmem,
        scratch_shapes=[
            pltpu.VMEM((SIDE + 2, SIDE + 2, 8, 256), F32),
            pltpu.VMEM((SIDE * SIDE, 128, 256), BF16),
            pltpu.VMEM((SIDE * SIDE, 256, 128), BF16),
            pltpu.VMEM((SIDE * SIDE, 4, 256), F32),
            pltpu.VMEM((4, 4, 8, 256), F32),
            pltpu.VMEM((count, 8, 256), F32),
            pltpu.VMEM((coarse_levels, leaf_total // 2 + 2, sub_total // 2 + 2, 8, 256), F32),
            pltpu.VMEM((2, 2, 2304, 256), BF16),
            pltpu.VMEM((coarse_levels, 2304, 128), BF16),
            dma,
            dma((coarse_levels,)),
            dma((8,)),
            dma((8,)),
            dma((8,)),
            dma((8,)),
            dma((count,)),
            dma((count,)),
        ],
        compiler_params=pltpu.CompilerParams(
            collective_id=0, has_side_effects=True, vmem_limit_bytes=40 * 1024 * 1024
        ),
    )(coords, vector, node_table, up, down, fine, coarse)


def solution(mesh):
    placed = (P(None, ("groups", "leaf"), "sub", None), P("rep", ("groups", "leaf"), "sub", None))
    return jax.shard_map(
        local,
        mesh=mesh,
        in_specs=placed,
        out_specs=P("rep", ("groups", "leaf"), "sub", None),
        check_vma=False,
    )
```

time: 135 us -> 50.7 us (0.38)
  Pallas kernels: 0 us -> 41.4 us
  blocking collectives: 37.8 us -> 0 us
  matrix products: 35.3 us -> 0 us
  starting transfers between devices: 20.7 us -> 0 us
  loops' own time: 11.1 us -> 0 us
  waiting for transfers between devices: 9.59 us -> 0 us
  other arithmetic: 7.78 us -> 0 us
  local copies, waits for them, and re-layouts: 10.3 us -> 8.9 us
    pallas_call x0 -> x1, Pallas kernels: none -> 41.4 us  [local(): pl.pallas_call(functools.partial(body, leaf_total, sub_total, coarse_leve...]
    dot_general x31 -> x0, matrix products: 35.3 us -> none  [the longest x4 22.6 us: near_leaf(): return jnp.einsum('cnb,nba->ca', source[3:], kernel, precision=HIGHEST)]
    all_gather x1 -> x0, blocking collectives: 34 us -> none  [local(): gathered = lax.all_gather(flat_moments, ('leaf', 'sub'), axis=0, tiled=True)]
    ppermute x8 -> x0, starting transfers between devices: 17.4 us -> none  [the longest x4 12 us: extended(): before = lax.ppermute(last, axis, up)]
    another operation x1 -> x0, loops' own time: 11.1 us -> none  [near_block(): lax.map(per_pair, jnp.arange(rows_here * pair_rows, dtype=jnp.int32))]
    ppermute x8 -> x0, waiting for transfers between devices: 8.25 us -> none  [the longest x4 8.24 us: extended(): after = lax.ppermute(leading, axis, down)]
    unnamed x104 -> x15, local copies, waits for them, and re-layouts: 3.43 us -> 8.9 us
    convert_element_type x4 -> x0, other arithmetic: 4.46 us -> none  [coupling_block(): (row_ok[row_shift][None, :, None] & col_ok[:, None, :]).astype(jnp.float32)]
  transfers between devices with their start and end apart: 9 -> 0, of which waited for: 3 -> 0; matrix products, arithmetic and copies ran while one was open for 15% -> 0% of each run, Pallas kernels for 0% -> 0%
where the time goes in v1:
time: 50.7 us; the launch traced here: 50.4 us
  Pallas kernels  41.4 us (82%)
  local copies, waits for them, and re-layouts  8.9 us (18%)
    pallas_call x1, Pallas kernels, local(): pl.pallas_call(functools.partial(body, leaf_total, sub_total, coarse_leve...  41.4 us
    unnamed x15, local copies, waits for them, and re-layouts  8.9 us

profile of v1, /device:TPU:0, one launch (start us, length us, event | category | flops | bytes accessed | tf_op | source)
XLA Modules:
  0.0 50.4 jit_solution(8833209492630771609)
XLA Ops:
  0.0 0.0 copy-start
  0.0 2.3 %copy-done = bf16[2,2,2304,256]{3,2,1,0:T(8,128)(2,1)S(1)} copy-done((bf16[2,2,2304,256]{3,2,1,0:T(8,128)(2,1)S(1)}, bf16[2,2,2304,256]{3,2,1,0:T(8,128)(2,1)}, u32[]{:S(2)}) %copy-start) | copy-done | bytes 4718616
  2.3 0.0 copy-start.1
  2.3 1.7 %copy-done.1 = bf16[1,4,2304,128]{3,2,1,0:T(8,128)(2,1)S(1)} copy-done((bf16[1,4,2304,128]{3,2,1,0:T(8,128)(2,1)S(1)}, bf16[1,4,2304,128]{3,2,1,0:T(8,128)(2,1)}, u32[]{:S(2)}) %copy-start.1) | copy-done | bytes 2359320
  4.0 0.0 copy-start.2
  4.0 0.9 %copy-done.2 = bf16[2,256,64]{2,1,0:T(8,128)(2,1)S(1)} copy-done((bf16[2,256,64]{2,1,0:T(8,128)(2,1)S(1)}, bf16[2,256,64]{2,1,0:T(8,128)(2,1)}, u32[]{:S(2)}) %copy-start.2) | copy-done | bytes 65560
  4.9 0.0 copy-start.3
  4.9 0.9 %copy-done.3 = f32[6,16,256]{2,1,0:T(8,128)S(1)} copy-done((f32[6,16,256]{2,1,0:T(8,128)S(1)}, f32[6,16,256]{2,1,0:T(8,128)}, u32[]{:S(2)}) %copy-start.3) | copy-done | bytes 98328
  5.8 0.0 copy-start.4
  5.8 0.8 %copy-done.4 = f32[4,4,4,256]{3,2,1,0:T(4,128)S(1)} copy-done((f32[4,4,4,256]{3,2,1,0:T(4,128)S(1)}, f32[4,4,4,256]{3,2,1,0:T(4,128)}, u32[]{:S(2)}) %copy-start.4) | copy-done | bytes 65560
  6.6 0.0 copy-start.5
  6.6 0.8 %copy-done.5 = bf16[2,64,256]{2,1,0:T(8,128)(2,1)S(1)} copy-done((bf16[2,64,256]{2,1,0:T(8,128)(2,1)S(1)}, bf16[2,64,256]{2,1,0:T(8,128)(2,1)}, u32[]{:S(2)}) %copy-start.5) | copy-done | bytes 65560
  7.5 0.0 copy-start.6
  7.5 0.8 %copy-done.6 = f32[3,4,4,256]{3,2,1,0:T(4,128)S(1)} copy-done((f32[3,4,4,256]{3,2,1,0:T(4,128)S(1)}, f32[3,4,4,256]{3,2,1,0:T(4,128)}, u32[]{:S(2)}) %copy-start.6) | copy-done | bytes 49176
  8.3 41.4 %shard_map.73 = f32[4,4,4,256]{3,2,1,0:T(4,128)S(1)} custom-call(f32[3,4,4,256]{3,2,1,0:T(4,128)S(1)} %copy-done.6, f32[4,4,4,256]{3,2,1,0:T(4,128)S(1)} %copy-done.4, f32[6,16,256]{2,1,0:T(8,128)S(1)} %copy-done.3, bf16[2,256,64]{2,1,0:T(8,128)(2,1)S(1)} %copy-done.2, bf16[2,64,256]{2,1,0:T(8,128)(2,1)S(1)} %copy-done.5, ...), custom_call_target="tpu_custom_call" | custom-call | tf_op jit(solution)/shard_map/pallas_call | solution.py:477
  49.7 0.6 %copy.9 = f32[4,4,4,256]{3,2,1,0:T(4,128)} copy(f32[4,4,4,256]{3,2,1,0:T(4,128)S(1)} %shard_map.73) | data formatting | bytes 131072
Async XLA Ops:
  0.0 2.3 %copy-start = (bf16[2,2,2304,256]{3,2,1,0:T(8,128)(2,1)S(1)}, bf16[2,2,2304,256]{3,2,1,0:T(8,128)(2,1)}, u32[]{:S(2)}) copy-start(bf16[2,2,2304,256]{3,2,1,0:T(8,128)(2,1)} %constant.13.clone.fine_hbm) | copy-start | bytes 14155780
  2.3 1.7 %copy-start.1 = (bf16[1,4,2304,128]{3,2,1,0:T(8,128)(2,1)S(1)}, bf16[1,4,2304,128]{3,2,1,0:T(8,128)(2,1)}, u32[]{:S(2)}) copy-start(bf16[1,4,2304,128]{3,2,1,0:T(8,128)(2,1)} %constant.14.clone.coarse_hbm) | copy-start | bytes 7077892
  4.0 0.9 %copy-start.2 = (bf16[2,256,64]{2,1,0:T(8,128)(2,1)S(1)}, bf16[2,256,64]{2,1,0:T(8,128)(2,1)}, u32[]{:S(2)}) copy-start(bf16[2,256,64]{2,1,0:T(8,128)(2,1)} %constant.11.clone.up_ref) | copy-start | bytes 196612
  4.9 0.9 %copy-start.3 = (f32[6,16,256]{2,1,0:T(8,128)S(1)}, f32[6,16,256]{2,1,0:T(8,128)}, u32[]{:S(2)}) copy-start(f32[6,16,256]{2,1,0:T(8,128)} %constant.10.clone.node_ref) | copy-start | bytes 294916
  5.8 0.8 %copy-start.4 = (f32[4,4,4,256]{3,2,1,0:T(4,128)S(1)}, f32[4,4,4,256]{3,2,1,0:T(4,128)}, u32[]{:S(2)}) copy-start(f32[4,4,4,256]{3,2,1,0:T(4,128)} %vector_ref.1) | copy-start | bytes 196612
  6.6 0.8 %copy-start.5 = (bf16[2,64,256]{2,1,0:T(8,128)(2,1)S(1)}, bf16[2,64,256]{2,1,0:T(8,128)(2,1)}, u32[]{:S(2)}) copy-start(bf16[2,64,256]{2,1,0:T(8,128)(2,1)} %constant.12.clone.down_ref) | copy-start | bytes 196612
  7.5 0.8 %copy-start.6 = (f32[3,4,4,256]{3,2,1,0:T(4,128)S(1)}, f32[3,4,4,256]{3,2,1,0:T(4,128)}, u32[]{:S(2)}) copy-start(f32[3,4,4,256]{3,2,1,0:T(4,128)} %coords_ref.1) | copy-start | bytes 147460

commit v2 on v1

--- a/solution.py
+++ b/solution.py
@@ -126,14 +126,19 @@
     leaf_total,
     sub_total,
     coarse_levels,
+    coords_hbm,
+    vector_hbm,
+    node_hbm,
+    up_hbm,
+    down_hbm,
+    fine_hbm,
+    coarse_hbm,
+    out_ref,
     coords_ref,
     vector_ref,
     node_ref,
     up_ref,
     down_ref,
-    fine_hbm,
-    coarse_hbm,
-    out_ref,
     pack,
     basis,
     flipped,
@@ -143,6 +148,7 @@
     level_mom,
     fine_w,
     coarse_w,
+    input_sem,
     weight_sem,
     coarse_sem,
     pack_send,
@@ -161,6 +167,20 @@
         other = lax.rem(me + step, count)
         return other, {"leaf": other // sub_total, "sub": lax.rem(other, sub_total)}
 
+    input_copies = [
+        pltpu.make_async_copy(src, dst, input_sem.at[k])
+        for k, (src, dst) in enumerate(
+            (
+                (coords_hbm, coords_ref),
+                (vector_hbm, vector_ref),
+                (node_hbm, node_ref),
+                (up_hbm, up_ref),
+                (down_hbm, down_ref),
+            )
+        )
+    ]
+    for copy in input_copies:
+        copy.start()
     fine_copy = pltpu.make_async_copy(fine_hbm, fine_w, weight_sem)
     fine_copy.start()
     coarse_copies = []
@@ -195,6 +215,8 @@
 
     lax.fori_loop(1, count, greet, 0)
 
+    input_copies[0].wait()
+    input_copies[1].wait()
     row_start = (leaf_at * SIDE).astype(F32) + 0.5
     col_start = (sub_at * SIDE).astype(F32) + 0.5
     for i in range(SIDE):
@@ -245,6 +267,8 @@
     pack_copies = halo(pack, SIDE, pack_send, pack_recv)
 
     nodes = np.array(poly_values(CHEB_NODES))
+    for copy in input_copies[2:]:
+        copy.wait()
     y_coefs = [node_ref[n] for n in range(3)]
     z_coefs = [node_ref[3 + n] for n in range(3)]
     row_id = lax.broadcasted_iota(jnp.int32, (8, 256), 0)
@@ -304,35 +328,38 @@
         sq = tile * tile
         return sq[0:1] + sq[1:2] + sq[2:3]
 
+    def flip(i, j):
+        box = pack[i, j]
+        first, second, third = parts_of(jnp.where(row_id < 3, box, 0.0))
+        n_first, n_second, n_third = parts_of(squares(box))
+        groups = []
+        for norm in (n_first, n_second, n_third):
+            tile = jnp.where(row_id == 3, ones, -2.0 * first)
+            groups.append(jnp.where(row_id == 4, norm, tile))
+        groups += [-2.0 * second, -2.0 * second, -2.0 * third]
+        groups.append(jnp.zeros((80, 256), F32))
+        flipped[i * (SIDE + 2) + j] = jnp.concatenate(groups, 0).T.astype(BF16)
+
     for i in range(SIDE):
         for j in range(SIDE):
-            box = pack[i + 1, j + 1]
-            first, second, third = parts_of(jnp.where(row_id < 3, box, 0.0))
-            n_first, n_second, n_third = parts_of(squares(box))
-            groups = []
-            for piece, norm in (
-                (first, n_first),
-                (first, n_second),
-                (first, n_third),
-            ):
-                tile = jnp.where(row_id == 3, ones, -2.0 * piece)
-                groups.append(jnp.where(row_id == 4, norm, tile))
-            groups += [-2.0 * second, -2.0 * second, -2.0 * third]
-            groups.append(jnp.zeros((80, 256), F32))
-            flipped[i * SIDE + j] = jnp.concatenate(groups, 0).T.astype(BF16)
-
+            flip(i + 1, j + 1)
     halo_wait(pack_copies)
+    for k in range(SIDE + 2):
+        flip(0, k)
+        flip(SIDE + 1, k)
+    for k in range(SIDE):
+        flip(k + 1, 0)
+        flip(k + 1, SIDE + 1)
 
     def near_box(box_at, carry):
         i = box_at // SIDE
         j = lax.rem(box_at, SIDE)
-        target = flipped[box_at][:, :48]
-        total = jnp.zeros((256, 16), F32)
+        target = pack[i + 1, j + 1]
+        total = jnp.zeros((16, 256), F32)
         for di in range(3):
             for dj in range(3):
-                box = pack[i + di, j + dj]
-                moved = jnp.where(row_id == 0, box + float(di - 1), box)
-                moved = jnp.where(row_id == 1, box + float(dj - 1), moved)
+                moved = jnp.where(row_id == 0, target + float(1 - di), target)
+                moved = jnp.where(row_id == 1, target + float(1 - dj), moved)
                 norm = squares(moved) + SMOOTHING
                 tile = jnp.where(row_id == 3, norm, jnp.where(row_id < 3, moved, 0.0))
                 first, second, third = parts_of(tile)
@@ -344,15 +371,18 @@
                     second,
                     first,
                 ]
-                source = jnp.concatenate(stacked, 0).astype(BF16)
-                v_high, v_low = halves(box[4:8])
+                feature = jnp.concatenate(stacked, 0).astype(BF16)
+                v_high, v_low = halves(pack[i + di, j + dj, 4:8])
                 vec = jnp.concatenate([v_high, v_low, jnp.zeros((8, 256), F32)], 0).astype(BF16)
-                kern = lax.rsqrt(mm(target, source))
-                high = kern.astype(BF16)
-                low = (kern - high.astype(F32)).astype(BF16)
-                total = total + mm_nt(high, vec) + mm_nt(low, vec)
-        wide = jnp.concatenate([total, jnp.zeros((256, 112), F32)], 1).T
-        near[box_at] = QUAD_WEIGHT * (wide[0:4] + wide[4:8])
+                source = (i + di) * (SIDE + 2) + j + dj
+                for half in range(2):
+                    part = slice(128 * half, 128 * half + 128)
+                    kern = lax.rsqrt(mm(flipped[source, part, :48], feature))
+                    high = kern.astype(BF16)
+                    low = (kern - high.astype(F32)).astype(BF16)
+                    weights = jnp.concatenate([high, low], 0)
+                    total = total + mm(jnp.concatenate([vec[:, part]] * 2, 1), weights)
+        near[box_at] = QUAD_WEIGHT * (total[0:4] + total[4:8])
         return carry
 
     lax.fori_loop(0, SIDE * SIDE, near_box, 0)
@@ -472,23 +502,29 @@
     coarse = np.stack(coarse)
 
     vmem = pl.BlockSpec(memory_space=pltpu.VMEM)
-    hbm = pl.BlockSpec(memory_space=pl.ANY)
+    hbm = pl.BlockSpec(memory_space=pltpu.HBM)
     dma = pltpu.SemaphoreType.DMA
     return pl.pallas_call(
         functools.partial(body, leaf_total, sub_total, coarse_levels),
         out_shape=jax.ShapeDtypeStruct(vector.shape, F32),
-        in_specs=[vmem, vmem, vmem, vmem, vmem, hbm, hbm],
+        in_specs=[hbm] * 7,
         out_specs=vmem,
         scratch_shapes=[
+            pltpu.VMEM(coords.shape, F32),
+            pltpu.VMEM(vector.shape, F32),
+            pltpu.VMEM(node_table.shape, F32),
+            pltpu.VMEM(up.shape, BF16),
+            pltpu.VMEM(down.shape, BF16),
             pltpu.VMEM((SIDE + 2, SIDE + 2, 8, 256), F32),
             pltpu.VMEM((SIDE * SIDE, 128, 256), BF16),
-            pltpu.VMEM((SIDE * SIDE, 256, 128), BF16),
+            pltpu.VMEM(((SIDE + 2) ** 2, 256, 128), BF16),
             pltpu.VMEM((SIDE * SIDE, 4, 256), F32),
             pltpu.VMEM((4, 4, 8, 256), F32),
             pltpu.VMEM((count, 8, 256), F32),
             pltpu.VMEM((coarse_levels, leaf_total // 2 + 2, sub_total // 2 + 2, 8, 256), F32),
             pltpu.VMEM((2, 2, 2304, 256), BF16),
             pltpu.VMEM((coarse_levels, 2304, 128), BF16),
+            dma((5,)),
             dma,
             dma((coarse_levels,)),
             dma((8,)),

time: 50.7 us -> 36.6 us (0.72)
  Pallas kernels: 41.4 us -> 27.3 us
    pallas_call x1, Pallas kernels: 41.4 us -> 27.3 us  [local(): pl.pallas_call(functools.partial(body, leaf_total, sub_total, coarse_leve...]
where the time goes in v2:
time: 36.6 us; the launch traced here: 36.2 us
  Pallas kernels  27.3 us (75%)
  local copies, waits for them, and re-layouts  8.9 us (24%)
    pallas_call x1, Pallas kernels, local(): pl.pallas_call(functools.partial(body, leaf_total, sub_total, coarse_leve...  27.3 us
    unnamed x15, local copies, waits for them, and re-layouts  8.9 us

profile of v2, /device:TPU:0, one launch (start us, length us, event | category | flops | bytes accessed | tf_op | source)
XLA Modules:
  0.0 36.2 jit_solution(7580368443228379479)
XLA Ops:
  0.0 0.0 copy-start
  0.0 2.3 %copy-done = bf16[2,2,2304,256]{3,2,1,0:T(8,128)(2,1)S(1)} copy-done((bf16[2,2,2304,256]{3,2,1,0:T(8,128)(2,1)S(1)}, bf16[2,2,2304,256]{3,2,1,0:T(8,128)(2,1)}, u32[]{:S(2)}) %copy-start) | copy-done | bytes 4718616
  2.3 0.0 copy-start.1
  2.3 1.7 %copy-done.1 = bf16[1,4,2304,128]{3,2,1,0:T(8,128)(2,1)S(1)} copy-done((bf16[1,4,2304,128]{3,2,1,0:T(8,128)(2,1)S(1)}, bf16[1,4,2304,128]{3,2,1,0:T(8,128)(2,1)}, u32[]{:S(2)}) %copy-start.1) | copy-done | bytes 2359320
  4.0 0.0 copy-start.2
  4.0 0.9 %copy-done.2 = bf16[2,256,64]{2,1,0:T(8,128)(2,1)S(1)} copy-done((bf16[2,256,64]{2,1,0:T(8,128)(2,1)S(1)}, bf16[2,256,64]{2,1,0:T(8,128)(2,1)}, u32[]{:S(2)}) %copy-start.2) | copy-done | bytes 65560
  4.9 0.0 copy-start.3
  4.9 0.9 %copy-done.3 = f32[6,16,256]{2,1,0:T(8,128)S(1)} copy-done((f32[6,16,256]{2,1,0:T(8,128)S(1)}, f32[6,16,256]{2,1,0:T(8,128)}, u32[]{:S(2)}) %copy-start.3) | copy-done | bytes 98328
  5.8 0.0 copy-start.4
  5.8 0.8 %copy-done.4 = f32[4,4,4,256]{3,2,1,0:T(4,128)S(1)} copy-done((f32[4,4,4,256]{3,2,1,0:T(4,128)S(1)}, f32[4,4,4,256]{3,2,1,0:T(4,128)}, u32[]{:S(2)}) %copy-start.4) | copy-done | bytes 65560
  6.6 0.0 copy-start.5
  6.6 0.8 %copy-done.5 = bf16[2,64,256]{2,1,0:T(8,128)(2,1)S(1)} copy-done((bf16[2,64,256]{2,1,0:T(8,128)(2,1)S(1)}, bf16[2,64,256]{2,1,0:T(8,128)(2,1)}, u32[]{:S(2)}) %copy-start.5) | copy-done | bytes 65560
  7.5 0.0 copy-start.6
  7.5 0.8 %copy-done.6 = f32[3,4,4,256]{3,2,1,0:T(4,128)S(1)} copy-done((f32[3,4,4,256]{3,2,1,0:T(4,128)S(1)}, f32[3,4,4,256]{3,2,1,0:T(4,128)}, u32[]{:S(2)}) %copy-start.6) | copy-done | bytes 49176
  8.3 27.3 %shard_map.73 = f32[4,4,4,256]{3,2,1,0:T(4,128)S(1)} custom-call(f32[3,4,4,256]{3,2,1,0:T(4,128)S(1)} %copy-done.6, f32[4,4,4,256]{3,2,1,0:T(4,128)S(1)} %copy-done.4, f32[6,16,256]{2,1,0:T(8,128)S(1)} %copy-done.3, bf16[2,256,64]{2,1,0:T(8,128)(2,1)S(1)} %copy-done.2, bf16[2,64,256]{2,1,0:T(8,128)(2,1)S(1)} %copy-done.5, ...), custom_call_target="tpu_custom_call" | custom-call | tf_op jit(solution)/shard_map/pallas_call | solution.py:507
  35.6 0.6 %copy.9 = f32[4,4,4,256]{3,2,1,0:T(4,128)} copy(f32[4,4,4,256]{3,2,1,0:T(4,128)S(1)} %shard_map.73) | data formatting | bytes 131072
Async XLA Ops:
  0.0 2.3 %copy-start = (bf16[2,2,2304,256]{3,2,1,0:T(8,128)(2,1)S(1)}, bf16[2,2,2304,256]{3,2,1,0:T(8,128)(2,1)}, u32[]{:S(2)}) copy-start(bf16[2,2,2304,256]{3,2,1,0:T(8,128)(2,1)} %constant.13.clone.fine_hbm) | copy-start | bytes 14155780
  2.3 1.7 %copy-start.1 = (bf16[1,4,2304,128]{3,2,1,0:T(8,128)(2,1)S(1)}, bf16[1,4,2304,128]{3,2,1,0:T(8,128)(2,1)}, u32[]{:S(2)}) copy-start(bf16[1,4,2304,128]{3,2,1,0:T(8,128)(2,1)} %constant.14.clone.coarse_hbm) | copy-start | bytes 7077892
  4.0 0.9 %copy-start.2 = (bf16[2,256,64]{2,1,0:T(8,128)(2,1)S(1)}, bf16[2,256,64]{2,1,0:T(8,128)(2,1)}, u32[]{:S(2)}) copy-start(bf16[2,256,64]{2,1,0:T(8,128)(2,1)} %constant.11.clone.up_hbm) | copy-start | bytes 196612
  4.9 0.9 %copy-start.3 = (f32[6,16,256]{2,1,0:T(8,128)S(1)}, f32[6,16,256]{2,1,0:T(8,128)}, u32[]{:S(2)}) copy-start(f32[6,16,256]{2,1,0:T(8,128)} %constant.10.clone.node_hbm) | copy-start | bytes 294916
  5.8 0.8 %copy-start.4 = (f32[4,4,4,256]{3,2,1,0:T(4,128)S(1)}, f32[4,4,4,256]{3,2,1,0:T(4,128)}, u32[]{:S(2)}) copy-start(f32[4,4,4,256]{3,2,1,0:T(4,128)} %vector_hbm.1) | copy-start | bytes 196612
  6.6 0.8 %copy-start.5 = (bf16[2,64,256]{2,1,0:T(8,128)(2,1)S(1)}, bf16[2,64,256]{2,1,0:T(8,128)(2,1)}, u32[]{:S(2)}) copy-start(bf16[2,64,256]{2,1,0:T(8,128)(2,1)} %constant.12.clone.down_hbm) | copy-start | bytes 196612
  7.5 0.8 %copy-start.6 = (f32[3,4,4,256]{3,2,1,0:T(4,128)S(1)}, f32[3,4,4,256]{3,2,1,0:T(4,128)}, u32[]{:S(2)}) copy-start(f32[3,4,4,256]{3,2,1,0:T(4,128)} %coords_hbm.1) | copy-start | bytes 147460

commit v3 on v2

--- a/solution.py
+++ b/solution.py
@@ -143,6 +143,7 @@
     basis,
     flipped,
     near,
+    near_out,
     mom,
     gathered,
     level_mom,
@@ -157,9 +158,14 @@
     mom_recv,
     all_send,
     all_recv,
+    partner_send,
+    partner_recv,
+    near_send,
+    near_recv,
 ):
     leaf_at = lax.axis_index("leaf")
     sub_at = lax.axis_index("sub")
+    rep_at = lax.axis_index("rep")
     me = leaf_at * sub_total + sub_at
     count = leaf_total * sub_total
 
@@ -196,10 +202,11 @@
 
     empty = jnp.zeros((8, 256), F32)
     for k in range(SIDE + 2):
-        pack[0, k] = empty
-        pack[SIDE + 1, k] = empty
-        pack[k, 0] = empty
-        pack[k, SIDE + 1] = empty
+        for slot in range(2):
+            pack[slot, 0, k] = empty
+            pack[slot, SIDE + 1, k] = empty
+            pack[slot, k, 0] = empty
+            pack[slot, k, SIDE + 1] = empty
     for k in range(4):
         mom[0, k] = empty
         mom[3, k] = empty
@@ -209,11 +216,17 @@
     barrier = pltpu.get_barrier_semaphore()
 
     def greet(step, carry):
-        _, where = peer(step)
+        at = lax.rem(2 * me + rep_at + step, 2 * count)
+        other = at // 2
+        where = {
+            "leaf": other // sub_total,
+            "sub": lax.rem(other, sub_total),
+            "rep": lax.rem(at, 2),
+        }
         pl.semaphore_signal(barrier, inc=1, device_id=where, device_id_type=MESH)
         return carry
 
-    lax.fori_loop(1, count, greet, 0)
+    lax.fori_loop(1, 2 * count, greet, 0)
 
     input_copies[0].wait()
     input_copies[1].wait()
@@ -221,14 +234,14 @@
     col_start = (sub_at * SIDE).astype(F32) + 0.5
     for i in range(SIDE):
         for j in range(SIDE):
-            pack[i + 1, j + 1, 0:1] = coords_ref[0, i, j : j + 1] - (row_start + float(i))
-            pack[i + 1, j + 1, 1:2] = coords_ref[1, i, j : j + 1] - (col_start + float(j))
-            pack[i + 1, j + 1, 2:3] = coords_ref[2, i, j : j + 1] - 0.5
-            pack[i + 1, j + 1, 3:4] = jnp.zeros((1, 256), F32)
+            pack[0, i + 1, j + 1, 0:1] = coords_ref[0, i, j : j + 1] - (row_start + float(i))
+            pack[0, i + 1, j + 1, 1:2] = coords_ref[1, i, j : j + 1] - (col_start + float(j))
+            pack[0, i + 1, j + 1, 2:3] = coords_ref[2, i, j : j + 1] - 0.5
+            pack[0, i + 1, j + 1, 3:4] = jnp.zeros((1, 256), F32)
             for c in range(4):
-                pack[i + 1, j + 1, 4 + c : 5 + c] = vector_ref[c, i, j : j + 1]
-
-    pl.semaphore_wait(barrier, count - 1)
+                pack[0, i + 1, j + 1, 4 + c : 5 + c] = vector_ref[c, i, j : j + 1]
+
+    pl.semaphore_wait(barrier, 2 * count - 1)
 
     def edge(inner, shift):
         if shift == 0:
@@ -264,7 +277,49 @@
             pl.when(to_ok)(copy.wait_send)
             pl.when(from_ok)(copy.wait_recv)
 
-    pack_copies = halo(pack, SIDE, pack_send, pack_recv)
+    partner_copy = pltpu.make_async_remote_copy(
+        src_ref=pack.at[0, pl.ds(2 - rep_at, 3), pl.ds(1, SIDE)],
+        dst_ref=pack.at[1, pl.ds(2 - rep_at, 3), pl.ds(1, SIDE)],
+        send_sem=partner_send,
+        recv_sem=partner_recv,
+        device_id={"rep": 1 - rep_at},
+        device_id_type=MESH,
+    )
+    partner_wait = pltpu.make_async_remote_copy(
+        src_ref=pack.at[0, pl.ds(1 + rep_at, 3), pl.ds(1, SIDE)],
+        dst_ref=pack.at[1, pl.ds(1 + rep_at, 3), pl.ds(1, SIDE)],
+        send_sem=partner_send,
+        recv_sem=partner_recv,
+        device_id={"rep": 1 - rep_at},
+        device_id_type=MESH,
+    )
+    pack_copies = []
+    for k, (di, dj) in enumerate(DIRECTIONS):
+        src_i, dst_i = edge(SIDE, di)
+        src_j, dst_j = edge(SIDE, dj)
+        to_ok = (leaf_at + di >= 0) & (leaf_at + di < leaf_total)
+        to_ok = to_ok & (sub_at + dj >= 0) & (sub_at + dj < sub_total)
+        from_ok = (leaf_at - di >= 0) & (leaf_at - di < leaf_total)
+        from_ok = from_ok & (sub_at - dj >= 0) & (sub_at - dj < sub_total)
+        for slot in range(2):
+            to_rep = lax.rem(rep_at + slot, 2)
+            goes, comes = to_ok, from_ok
+            if di != 0:
+                taker = 1 if di < 0 else 0
+                goes = goes & (to_rep == taker)
+                comes = comes & (rep_at == taker)
+            copy = pltpu.make_async_remote_copy(
+                src_ref=pack.at[0, src_i, src_j],
+                dst_ref=pack.at[slot, dst_i, dst_j],
+                send_sem=pack_send.at[k, slot],
+                recv_sem=pack_recv.at[k, slot],
+                device_id={"leaf": leaf_at + di, "sub": sub_at + dj, "rep": to_rep},
+                device_id_type=MESH,
+            )
+            pack_copies.append((copy, goes, comes))
+    for copy, goes, _ in pack_copies:
+        pl.when(goes)(copy.start)
+    partner_copy.start()
 
     nodes = np.array(poly_values(CHEB_NODES))
     for copy in input_copies[2:]:
@@ -274,7 +329,7 @@
     row_id = lax.broadcasted_iota(jnp.int32, (8, 256), 0)
     for i in range(SIDE):
         for j in range(SIDE):
-            box = pack[i + 1, j + 1]
+            box = pack[0, i + 1, j + 1]
             y_part = wide_node(2.0 * box[1:2], y_coefs)
             z_part = wide_node(2.0 * box[2:3], z_coefs)
             yz_part = y_part * z_part
@@ -329,7 +384,7 @@
         return sq[0:1] + sq[1:2] + sq[2:3]
 
     def flip(i, j):
-        box = pack[i, j]
+        box = pack[0, i, j]
         first, second, third = parts_of(jnp.where(row_id < 3, box, 0.0))
         n_first, n_second, n_third = parts_of(squares(box))
         groups = []
@@ -340,21 +395,22 @@
         groups.append(jnp.zeros((80, 256), F32))
         flipped[i * (SIDE + 2) + j] = jnp.concatenate(groups, 0).T.astype(BF16)
 
-    for i in range(SIDE):
+    for k in range(3):
         for j in range(SIDE):
-            flip(i + 1, j + 1)
+            flip(1 + rep_at + k, j + 1)
     halo_wait(pack_copies)
-    for k in range(SIDE + 2):
-        flip(0, k)
-        flip(SIDE + 1, k)
-    for k in range(SIDE):
-        flip(k + 1, 0)
-        flip(k + 1, SIDE + 1)
+    partner_copy.wait_send()
+    partner_wait.wait_recv()
+    for j in range(SIDE + 2):
+        flip(5 * rep_at, j)
+    for k in range(3):
+        flip(1 + rep_at + k, 0)
+        flip(1 + rep_at + k, SIDE + 1)
 
     def near_box(box_at, carry):
         i = box_at // SIDE
         j = lax.rem(box_at, SIDE)
-        target = pack[i + 1, j + 1]
+        target = pack[0, i + 1, j + 1]
         total = jnp.zeros((16, 256), F32)
         for di in range(3):
             for dj in range(3):
@@ -372,8 +428,11 @@
                     first,
                 ]
                 feature = jnp.concatenate(stacked, 0).astype(BF16)
-                v_high, v_low = halves(pack[i + di, j + dj, 4:8])
-                vec = jnp.concatenate([v_high, v_low, jnp.zeros((8, 256), F32)], 0).astype(BF16)
+                vec = rows_of_halves(
+                    jnp.concatenate(
+                        [pack[0, i + di, j + dj, 4:8], pack[1, i + di, j + dj, 4:8]], 0
+                    )
+                )
                 source = (i + di) * (SIDE + 2) + j + dj
                 for half in range(2):
                     part = slice(128 * half, 128 * half + 128)
@@ -382,10 +441,26 @@
                     low = (kern - high.astype(F32)).astype(BF16)
                     weights = jnp.concatenate([high, low], 0)
                     total = total + mm(jnp.concatenate([vec[:, part]] * 2, 1), weights)
-        near[box_at] = QUAD_WEIGHT * (total[0:4] + total[4:8])
+        result = QUAD_WEIGHT * (total[0:8] + total[8:16])
+        near[box_at] = result[0:4]
+        near_out[box_at] = result[4:8]
         return carry
 
-    lax.fori_loop(0, SIDE * SIDE, near_box, 0)
+    def near_copy(row, step):
+        at = pl.ds(SIDE * row, SIDE)
+        return pltpu.make_async_remote_copy(
+            src_ref=near_out.at[at],
+            dst_ref=near.at[at],
+            send_sem=near_send.at[step],
+            recv_sem=near_recv.at[step],
+            device_id={"rep": 1 - rep_at},
+            device_id_type=MESH,
+        )
+
+    for step in range(2):
+        row = 2 * rep_at + step
+        lax.fori_loop(SIDE * row, SIDE * row + SIDE, near_box, 0)
+        near_copy(row, step).start()
 
     def spread_wait(step, carry):
         spread_copy(step, True).wait_send()
@@ -463,6 +538,9 @@
     level_zero = mm_split(stacked, down_ref[0], down_ref[1]) + mm_split(
         window, fine_w[0, 0], fine_w[0, 1]
     )
+    for step in range(2):
+        near_copy(2 * rep_at + step, step).wait_send()
+        near_copy(2 - 2 * rep_at + step, step).wait_recv()
     for i in range(SIDE):
         for j in range(SIDE):
             row = 8 * (2 * (i // 2) + j // 2)
@@ -515,9 +593,10 @@
             pltpu.VMEM(node_table.shape, F32),
             pltpu.VMEM(up.shape, BF16),
             pltpu.VMEM(down.shape, BF16),
-            pltpu.VMEM((SIDE + 2, SIDE + 2, 8, 256), F32),
+            pltpu.VMEM((2, SIDE + 2, SIDE + 2, 8, 256), F32),
             pltpu.VMEM((SIDE * SIDE, 128, 256), BF16),
             pltpu.VMEM(((SIDE + 2) ** 2, 256, 128), BF16),
+            pltpu.VMEM((SIDE * SIDE, 4, 256), F32),
             pltpu.VMEM((SIDE * SIDE, 4, 256), F32),
             pltpu.VMEM((4, 4, 8, 256), F32),
             pltpu.VMEM((count, 8, 256), F32),
@@ -527,15 +606,19 @@
             dma((5,)),
             dma,
             dma((coarse_levels,)),
-            dma((8,)),
-            dma((8,)),
+            dma((8, 2)),
+            dma((8, 2)),
             dma((8,)),
             dma((8,)),
             dma((count,)),
             dma((count,)),
+            dma,
+            dma,
+            dma((2,)),
+            dma((2,)),
         ],
         compiler_params=pltpu.CompilerParams(
-            collective_id=0, has_side_effects=True, vmem_limit_bytes=40 * 1024 * 1024
+            collective_id=0, has_side_effects=True, vmem_limit_bytes=60 * 1024 * 1024
         ),
     )(coords, vector, node_table, up, down, fine, coarse)
 

time: 36.6 us -> 22.5 us (0.61)
  the two profiles are of different devices: /device:TPU:0 before, /device:TPU:1 now
where the time goes in v3:
time: 22.5 us; the launch traced here: 22.4 us
  Pallas kernels  20.9 us (93%)
  local copies, waits for them, and re-layouts  1.47 us (7%)
    pallas_call x1, Pallas kernels, local(): pl.pallas_call(functools.partial(body, leaf_total, sub_total, coarse_leve...  20.9 us
    unnamed x1, local copies, waits for them, and re-layouts  1.47 us

profile of v3, /device:TPU:1, one launch (start us, length us, event | category | flops | bytes accessed | tf_op | source)
XLA Modules:
  0.0 22.4 jit_solution(5325588359835719868)
XLA Ops:
  0.0 20.9 %shard_map.73 = f32[4,4,4,256]{3,2,1,0:T(4,128)} custom-call(f32[3,4,4,256]{3,2,1,0:T(4,128)} %coords_hbm.1, f32[4,4,4,256]{3,2,1,0:T(4,128)} %vector_hbm.1, f32[6,16,256]{2,1,0:T(8,128)} %constant.10.clone.node_hbm, bf16[2,256,64]{2,1,0:T(8,128)(2,1)} %constant.11.clone.up_hbm, bf16[2,64,256]{2,1,0:T(8,128)(2,1)} %constant.12.clone.down_hbm, ...), custom_call_target="tpu_custom_call" | custom-call | tf_op jit(solution)/shard_map/pallas_call | solution.py:585
  20.9 1.5 %copy.9 = f32[4,4,4,256]{3,2,1,0:T(4,128)} copy(f32[4,4,4,256]{3,2,1,0:T(4,128)} %shard_map.73) | data formatting | bytes 131072

commit v4 on v3

--- a/solution.py
+++ b/solution.py
@@ -144,6 +144,7 @@
     flipped,
     near,
     near_out,
+    sums,
     mom,
     gathered,
     level_mom,
@@ -398,53 +399,79 @@
     for k in range(3):
         for j in range(SIDE):
             flip(1 + rep_at + k, j + 1)
-    halo_wait(pack_copies)
     partner_copy.wait_send()
     partner_wait.wait_recv()
+
+    def pair(i, j, row, col):
+        target = pack[0, i + 1, j + 1]
+        moved = jnp.where(row_id == 0, target + (i + 1 - row).astype(F32), target)
+        moved = jnp.where(row_id == 1, target + float(j + 1 - col), moved)
+        norm = squares(moved) + SMOOTHING
+        tile = jnp.where(row_id == 3, norm, jnp.where(row_id < 3, moved, 0.0))
+        first, second, third = parts_of(tile)
+        stacked = [
+            jnp.where(row_id == 4, ones, first),
+            jnp.where(row_id == 4, ones, second),
+            jnp.where(row_id == 4, ones, third),
+            first,
+            second,
+            first,
+        ]
+        feature = jnp.concatenate(stacked, 0).astype(BF16)
+        vec = rows_of_halves(
+            jnp.concatenate([pack[0, row, col, 4:8], pack[1, row, col, 4:8]], 0)
+        )
+        source = row * (SIDE + 2) + col
+        total = jnp.zeros((16, 256), F32)
+        for half in range(2):
+            part = slice(128 * half, 128 * half + 128)
+            kern = lax.rsqrt(mm(flipped[source, part, :48], feature))
+            high = kern.astype(BF16)
+            low = (kern - high.astype(F32)).astype(BF16)
+            weights = jnp.concatenate([high, low], 0)
+            total = total + mm(jnp.concatenate([vec[:, part]] * 2, 1), weights)
+        return total
+
+    def own_rows(t):
+        outer = t // 3
+        i = outer * 3 * rep_at + (1 - outer) * (1 + rep_at)
+        row = outer * (1 + 2 * rep_at + t - 3) + (1 - outer) * (1 + rep_at + t)
+        step = (outer + 1 + rep_at) % 2
+        return i, row, step
+
+    for k in range(2):
+        for j in range(SIDE):
+            sums[k, j] = jnp.zeros((16, 256), F32)
+
+    def own_pairs(t, carry):
+        i, row, step = own_rows(t)
+        for j in range(SIDE):
+            total = sums[step, j]
+            for col in range(max(j, 1), min(j + 3, SIDE + 1)):
+                total = total + pair(i, j, row, col)
+            sums[step, j] = total
+        return carry
+
+    lax.fori_loop(0, 5, own_pairs, 0)
+    halo_wait(pack_copies)
     for j in range(SIDE + 2):
         flip(5 * rep_at, j)
     for k in range(3):
         flip(1 + rep_at + k, 0)
         flip(1 + rep_at + k, SIDE + 1)
 
-    def near_box(box_at, carry):
-        i = box_at // SIDE
-        j = lax.rem(box_at, SIDE)
-        target = pack[0, i + 1, j + 1]
-        total = jnp.zeros((16, 256), F32)
-        for di in range(3):
-            for dj in range(3):
-                moved = jnp.where(row_id == 0, target + float(1 - di), target)
-                moved = jnp.where(row_id == 1, target + float(1 - dj), moved)
-                norm = squares(moved) + SMOOTHING
-                tile = jnp.where(row_id == 3, norm, jnp.where(row_id < 3, moved, 0.0))
-                first, second, third = parts_of(tile)
-                stacked = [
-                    jnp.where(row_id == 4, ones, first),
-                    jnp.where(row_id == 4, ones, second),
-                    jnp.where(row_id == 4, ones, third),
-                    first,
-                    second,
-                    first,
-                ]
-                feature = jnp.concatenate(stacked, 0).astype(BF16)
-                vec = rows_of_halves(
-                    jnp.concatenate(
-                        [pack[0, i + di, j + dj, 4:8], pack[1, i + di, j + dj, 4:8]], 0
-                    )
-                )
-                source = (i + di) * (SIDE + 2) + j + dj
-                for half in range(2):
-                    part = slice(128 * half, 128 * half + 128)
-                    kern = lax.rsqrt(mm(flipped[source, part, :48], feature))
-                    high = kern.astype(BF16)
-                    low = (kern - high.astype(F32)).astype(BF16)
-                    weights = jnp.concatenate([high, low], 0)
-                    total = total + mm(jnp.concatenate([vec[:, part]] * 2, 1), weights)
-        result = QUAD_WEIGHT * (total[0:8] + total[8:16])
-        near[box_at] = result[0:4]
-        near_out[box_at] = result[4:8]
+    def side_pairs(t, carry):
+        i, row, step = own_rows(t)
+        sums[step, 0] += pair(i, 0, row, 0)
+        sums[step, SIDE - 1] += pair(i, SIDE - 1, row, SIDE + 1)
         return carry
+
+    lax.fori_loop(0, 5, side_pairs, 0)
+    for j in range(SIDE):
+        total = sums[rep_at, j]
+        for col in range(j, j + 3):
+            total = total + pair(3 * rep_at, j, 5 * rep_at, col)
+        sums[rep_at, j] = total
 
     def near_copy(row, step):
         at = pl.ds(SIDE * row, SIDE)
@@ -459,7 +486,11 @@
 
     for step in range(2):
         row = 2 * rep_at + step
-        lax.fori_loop(SIDE * row, SIDE * row + SIDE, near_box, 0)
+        for j in range(SIDE):
+            total = sums[step, j]
+            result = QUAD_WEIGHT * (total[0:8] + total[8:16])
+            near[SIDE * row + j] = result[0:4]
+            near_out[SIDE * row + j] = result[4:8]
         near_copy(row, step).start()
 
     def spread_wait(step, carry):
@@ -598,6 +629,7 @@
             pltpu.VMEM(((SIDE + 2) ** 2, 256, 128), BF16),
             pltpu.VMEM((SIDE * SIDE, 4, 256), F32),
             pltpu.VMEM((SIDE * SIDE, 4, 256), F32),
+            pltpu.VMEM((2, SIDE, 16, 256), F32),
             pltpu.VMEM((4, 4, 8, 256), F32),
             pltpu.VMEM((count, 8, 256), F32),
             pltpu.VMEM((coarse_levels, leaf_total // 2 + 2, sub_total // 2 + 2, 8, 256), F32),

time: 22.5 us -> 21.5 us (0.956)
  the two profiles are of different devices: /device:TPU:1 before, /device:TPU:0 now
where the time goes in v4:
time: 21.5 us; the launch traced here: 21.3 us
  Pallas kernels  19.9 us (93%)
  local copies, waits for them, and re-layouts  1.47 us (7%)
    pallas_call x1, Pallas kernels, local(): pl.pallas_call(functools.partial(body, leaf_total, sub_total, coarse_leve...  19.9 us
    unnamed x1, local copies, waits for them, and re-layouts  1.47 us

profile of v4, /device:TPU:0, one launch (start us, length us, event | category | flops | bytes accessed | tf_op | source)
XLA Modules:
  0.0 21.3 jit_solution(15008611338443857537)
XLA Ops:
  0.0 19.9 %shard_map.73 = f32[4,4,4,256]{3,2,1,0:T(4,128)} custom-call(f32[3,4,4,256]{3,2,1,0:T(4,128)} %coords_hbm.1, f32[4,4,4,256]{3,2,1,0:T(4,128)} %vector_hbm.1, f32[6,16,256]{2,1,0:T(8,128)} %constant.10.clone.node_hbm, bf16[2,256,64]{2,1,0:T(8,128)(2,1)} %constant.11.clone.up_hbm, bf16[2,64,256]{2,1,0:T(8,128)(2,1)} %constant.12.clone.down_hbm, ...), custom_call_target="tpu_custom_call" | custom-call | tf_op jit(solution)/shard_map/pallas_call | solution.py:616
  19.9 1.5 %copy.9 = f32[4,4,4,256]{3,2,1,0:T(4,128)} copy(f32[4,4,4,256]{3,2,1,0:T(4,128)} %shard_map.73) | data formatting | bytes 131072

commit v5 on v4

--- a/solution.py
+++ b/solution.py
@@ -294,6 +294,7 @@
         device_id={"rep": 1 - rep_at},
         device_id_type=MESH,
     )
+    partner_copy.start()
     pack_copies = []
     for k, (di, dj) in enumerate(DIRECTIONS):
         src_i, dst_i = edge(SIDE, di)
@@ -320,7 +321,6 @@
             pack_copies.append((copy, goes, comes))
     for copy, goes, _ in pack_copies:
         pl.when(goes)(copy.start)
-    partner_copy.start()
 
     nodes = np.array(poly_values(CHEB_NODES))
     for copy in input_copies[2:]:

time: 21.5 us -> 21.5 us (level)
  no operation moved by 1% of the time
where the time goes in v5:
time: 21.5 us; the launch traced here: 21.3 us
  Pallas kernels  19.9 us (93%)
  local copies, waits for them, and re-layouts  1.47 us (7%)
    pallas_call x1, Pallas kernels, local(): pl.pallas_call(functools.partial(body, leaf_total, sub_total, coarse_leve...  19.9 us
    unnamed x1, local copies, waits for them, and re-layouts  1.47 us

profile of v5, /device:TPU:0, one launch (start us, length us, event | category | flops | bytes accessed | tf_op | source)
XLA Modules:
  0.0 21.3 jit_solution(7289601359353406798)
XLA Ops:
  0.0 19.9 %shard_map.73 = f32[4,4,4,256]{3,2,1,0:T(4,128)} custom-call(f32[3,4,4,256]{3,2,1,0:T(4,128)} %coords_hbm.1, f32[4,4,4,256]{3,2,1,0:T(4,128)} %vector_hbm.1, f32[6,16,256]{2,1,0:T(8,128)} %constant.10.clone.node_hbm, bf16[2,256,64]{2,1,0:T(8,128)(2,1)} %constant.11.clone.up_hbm, bf16[2,64,256]{2,1,0:T(8,128)(2,1)} %constant.12.clone.down_hbm, ...), custom_call_target="tpu_custom_call" | custom-call | tf_op jit(solution)/shard_map/pallas_call | solution.py:616
  19.9 1.5 %copy.9 = f32[4,4,4,256]{3,2,1,0:T(4,128)} copy(f32[4,4,4,256]{3,2,1,0:T(4,128)} %shard_map.73) | data formatting | bytes 131072
